TPU v7x, 32 devices: a whole 2x2x4 slice. The times are simulated.
32 devices in a mesh: seq: 16 (over z, y, x), head: 2 (over core).
Axes of the slice: x: 2, y: 2, z: 4, core: 2. Of those that a mesh axis runs over, the one named last changes fastest.
Arguments:
- block_input: bfloat16 [2048, 1024], P('seq'), may hold values from -7 to 7
- first_layer_value: bfloat16 [2048, 1024], P('seq', 'head'), may hold values from -6 to 6
- output_gradient: bfloat16 [2048, 1024], P('seq'), may hold values from -6 to 6
- segment_index: int32 [128], replicated, may hold values from 0 to 2, as said below
- channel_parameters: bfloat16 [11, 1024], P(None, 'seq'), may hold values from -1 to 1.5
- head_parameters: bfloat16 [8, 1024], P(None, ('head', 'seq')), may hold values from -11 to 3
- mixing_weights: bfloat16 [3, 1024, 1024], P(None, 'seq', 'head'), may hold values from -0.1875 to 0.1875
- output_weight: bfloat16 [1024, 1024], P('head', 'seq'), may hold values from -0.1875 to 0.1875
- low_rank_down_weight: bfloat16 [1024, 288], P('seq'), may hold values from -0.1875 to 0.1875
- low_rank_up_weight: bfloat16 [288, 1024], P(None, ('head', 'seq')), may hold values from -0.75 to 0.75
- channel_key_matrix: bfloat16 [1024, 4096], P('seq', 'head'), may hold values from -0.1875 to 0.1875
- channel_value_matrix: bfloat16 [4096, 1024], P('head', 'seq'), may hold values from -0.09375 to 0.09375
Outputs:
- block_out: bfloat16 [2048, 1024], P('seq')
- grad_block_in: float32 [2048, 1024], P('seq')
- grad_value_first: float32 [2048, 1024], P('seq', 'head')
- grad_chan_params: float32 [11, 1024], P(None, 'seq')
- grad_head_params: float32 [8, 1024], P(None, ('head', 'seq'))
- grad_mix_weights: float32 [3, 1024, 1024], P(None, 'seq', 'head')
- grad_out_weights: float32 [1024, 1024], P('head', 'seq')
- grad_lora_down: float32 [1024, 288], P('seq')
- grad_lora_up: float32 [288, 1024], P(None, ('head', 'seq'))
- grad_channel_key: float32 [1024, 4096], P('seq', 'head')
- grad_channel_value: float32 [4096, 1024], P('head', 'seq')
Inputs may be any that keep to these rules, and one draw needn't show every extreme that they name: `segment_index`: ids never fall; ids 0 and 2 each hold at least one block and lie within the first and the last 8 blocks.
All inputs are finite; a program needn't handle non-finite values.
Results may differ from a plain program's by a relative error of at most 0.009.
The roundings to bfloat16 on the way count: a program that leaves them out, or rounds other values in their place, can miss the bound.
Values may be sent and summed in bfloat16 or wider, within the bound.
A program may use at most 256 MiB of HBM per device.

v0:
```python
from functools import partial

import jax
import jax.numpy as jnp
from jax import lax
from jax.sharding import PartitionSpec as P

ATTEND_DIM = 64
DECAY_LOW_RANK = 64
RATE_RANK = 64
VALUE_RANK = 32
BLK = 16


PRECISE = lax.Precision.HIGHEST


def from_behind(value, axis, steps):
    count = lax.axis_size(axis)
    initial, last = (max(0, -steps), min(count, count - steps))
    return lax.ppermute(value, axis, [(source, source + steps) for source in range(initial, last)])


def prefix(part, axis, combine, identity, reverse):
    count = lax.axis_size(axis)
    place = lax.axis_index(axis)
    ahead = count - 1 - place if reverse else place
    gathered = jax.tree.map(lambda a: lax.all_gather(a, axis), part)
    state = jax.tree.map(lambda a, e: jnp.zeros_like(a) + jnp.asarray(e, a.dtype), part, identity)

    def one(step, state):
        source = count - 1 - step if reverse else step
        return combine(
            state, jax.tree.map(lambda a: lax.dynamic_index_in_dim(a, source, 0, False), gathered)
        )

    return lax.fori_loop(0, ahead, one, state)


def product_matrix(operand, weights):
    return jnp.dot(operand, weights, preferred_element_type=jnp.float32)


def back_product(gradient, weights):
    return lax.dot_general(
        gradient, weights, (((1,), (1,)), ((), ())), preferred_element_type=jnp.float32
    )


def weight_grad(operand, gradient):
    return lax.dot_general(
        operand, gradient, (((0,), (0,)), ((), ())), preferred_element_type=jnp.float32
    )


def layer_norm(value_rows, scale_vec, offset_vec):
    centre = value_rows - jnp.mean(value_rows, axis=-1, keepdims=True)
    spread = jnp.mean(centre * centre, axis=-1, keepdims=True)
    return centre * lax.rsqrt(spread + 1e-05) * scale_vec + offset_vec


def prepare_inputs(
    receptance_unscaled,
    key_unscaled,
    value_unscaled,
    decay_low_rank,
    rate_low_rank,
    value_low_rank,
    first_layer_value,
    attend_elements,
):
    rows_here = receptance_unscaled.shape[0]
    attend_count = receptance_unscaled.shape[1] // ATTEND_DIM
    logarithm_scale = -jax.nn.softplus(-(attend_elements[0] + decay_low_rank)) - 0.5
    log_decay = -jnp.exp(logarithm_scale)
    rate_sigmoid = jax.nn.sigmoid(attend_elements[1] + rate_low_rank)
    payload_blended = value_unscaled + (first_layer_value - value_unscaled) * jax.nn.sigmoid(
        attend_elements[2] + value_low_rank
    )
    scaled = (key_unscaled * attend_elements[3]).reshape(rows_here, attend_count, ATTEND_DIM)
    unit_key = scaled * lax.rsqrt(jnp.sum(scaled * scaled, axis=-1, keepdims=True) + 1e-05)
    lookup_used = key_unscaled * (1.0 + (rate_sigmoid - 1.0) * attend_elements[4])
    layout = (rows_here, attend_count, ATTEND_DIM)
    return (
        receptance_unscaled.reshape(layout),
        log_decay.reshape(layout),
        -unit_key,
        unit_key * rate_sigmoid.reshape(layout),
        lookup_used.reshape(layout),
        payload_blended.reshape(layout),
    )


def finish(
    read_out, reader_vectors, lookup_used, payload_blended, gate_activation, attend_elements
):
    rows_here, attend_count, _ = read_out.shape
    centre = read_out - jnp.mean(read_out, axis=-1, keepdims=True)
    unit_length_vectors = centre * lax.rsqrt(
        jnp.mean(centre * centre, axis=-1, keepdims=True) + 0.00064
    )
    extra_addend = (
        jnp.sum(
            reader_vectors * lookup_used * attend_elements[5].reshape(attend_count, ATTEND_DIM),
            axis=-1,
            keepdims=True,
        )
        * payload_blended
    )
    final_answer = (
        unit_length_vectors * attend_elements[6].reshape(attend_count, ATTEND_DIM)
        + attend_elements[7].reshape(attend_count, ATTEND_DIM)
        + extra_addend
    )
    return final_answer.reshape(rows_here, attend_count * ATTEND_DIM) * gate_activation


def recurrence(reader_vectors, log_decay, removal, refill, lookup_used, payload_blended, keep):
    rows_here, attend_count, head_width = reader_vectors.shape
    block_count = rows_here // BLK

    def arrange(value_rows):
        return jnp.transpose(
            value_rows.reshape(block_count, BLK, attend_count, value_rows.shape[2]), (0, 2, 1, 3)
        )

    padded_value = jnp.concatenate([payload_blended, jnp.zeros_like(payload_blended)], axis=2)
    feeds = (
        arrange(reader_vectors),
        arrange(log_decay),
        arrange(removal),
        arrange(refill),
        arrange(lookup_used),
        arrange(padded_value),
        keep,
    )
    strict = (jnp.arange(BLK)[:, None] > jnp.arange(BLK)[None, :]).astype(jnp.float32)[None]
    inclusive = (jnp.arange(BLK)[:, None] >= jnp.arange(BLK)[None, :]).astype(jnp.float32)[None]
    unit_block = jnp.eye(BLK, dtype=jnp.float32)[None]
    identity_rows = jnp.broadcast_to(
        jnp.eye(head_width, dtype=jnp.float32), (attend_count, head_width, head_width)
    )
    initial = jnp.concatenate([jnp.zeros_like(identity_rows), identity_rows], axis=1)

    def advance(memory, inputs_now):
        recv_now, decay_now, removal_now, refill_now, key_now, value_now, keep_now = inputs_now
        memory = memory * keep_now
        cumulative = jnp.cumsum(decay_now, axis=1)
        exclusive = cumulative - decay_now
        growth = jnp.exp(-cumulative)
        refill_grown = refill_now * growth
        key_grown = key_now * growth
        first_term = removal_now * jnp.exp(exclusive)
        reader_term = recv_now * jnp.exp(cumulative)
        mix_refill = (
            jnp.einsum("htj,hsj->hts", first_term, refill_grown, precision=PRECISE) * strict
        )
        mix_key = jnp.einsum("htj,hsj->hts", first_term, key_grown, precision=PRECISE) * strict
        right_side = jnp.einsum("htj,hij->hti", first_term, memory, precision=PRECISE) + jnp.einsum(
            "hts,hsi->hti", mix_key, value_now, precision=PRECISE
        )
        inverse = unit_block + mix_refill
        power = mix_refill
        for _ in range(BLK.bit_length() - 2):
            power = jnp.einsum("hts,hsu->htu", power, power, precision=PRECISE)
            inverse = inverse + jnp.einsum("hts,hsu->htu", inverse, power, precision=PRECISE)
        removed = jnp.einsum("hts,hsi->hti", inverse, right_side, precision=PRECISE)
        read_refill = (
            jnp.einsum("htj,hsj->hts", reader_term, refill_grown, precision=PRECISE) * inclusive
        )
        read_key = jnp.einsum("htj,hsj->hts", reader_term, key_grown, precision=PRECISE) * inclusive
        output = (
            jnp.einsum("htj,hij->hti", reader_term, memory, precision=PRECISE)
            + jnp.einsum("hts,hsi->hti", read_refill, removed, precision=PRECISE)
            + jnp.einsum("hts,hsi->hti", read_key, value_now, precision=PRECISE)
        )
        total = cumulative[:, BLK - 1 :, :]
        tail = jnp.exp(total - cumulative)
        memory = (
            memory * jnp.exp(total)
            + jnp.einsum("hsi,hsj->hij", removed, refill_now * tail, precision=PRECISE)
            + jnp.einsum("hsi,hsj->hij", value_now, key_now * tail, precision=PRECISE)
        )
        return (memory, output)

    final, outputs = lax.scan(advance, initial, feeds)
    outputs = jnp.transpose(outputs, (0, 2, 1, 3)).reshape(rows_here, attend_count, 2 * head_width)
    return (
        outputs[:, :, :head_width],
        outputs[:, :, head_width:],
        final[:, :head_width],
        final[:, head_width:],
    )


def compose(earlier, later):
    first_map, first_add = earlier
    second_map, second_add = later
    return (
        jnp.einsum("hij,hjk->hik", first_map, second_map, precision=PRECISE),
        jnp.einsum("hij,hjk->hik", first_add, second_map, precision=PRECISE) + second_add,
    )


def shards(
    block_input,
    first_layer_value,
    output_gradient,
    segment_index,
    channel_parameters,
    head_parameters,
    mixing_weights,
    output_weight,
    low_rank_down_weight,
    low_rank_up_weight,
    channel_key_matrix,
    channel_value_matrix,
):
    gathered = (
        lax.all_gather(mixing_weights, "seq", axis=1, tiled=True),
        lax.all_gather(output_weight, "seq", axis=1, tiled=True),
        lax.all_gather(low_rank_down_weight, "seq", axis=0, tiled=True),
        lax.all_gather(low_rank_up_weight, "seq", axis=1, tiled=True),
        lax.all_gather(channel_key_matrix, "seq", axis=0, tiled=True),
        lax.all_gather(channel_value_matrix, "seq", axis=1, tiled=True),
        lax.all_gather(head_parameters, "seq", axis=1, tiled=True),
        lax.all_gather(channel_parameters, "seq", axis=1, tiled=True),
    )
    (
        mix_full,
        out_full,
        down_full,
        upper_triangle_full,
        key_full,
        value_full,
        head_full,
        chan_full,
    ) = gathered
    chan_vals = chan_full.astype(jnp.float32)
    attend_elements = head_full.astype(jnp.float32)
    first_boundary = DECAY_LOW_RANK
    second_boundary = first_boundary + RATE_RANK
    third_boundary = second_boundary + VALUE_RANK
    rows_here = block_input.shape[0]
    attend_count = head_full.shape[1] // ATTEND_DIM
    block_count = rows_here // BLK
    place = lax.axis_index("seq")
    earlier_id = jnp.where(
        place > 0,
        lax.dynamic_slice_in_dim(segment_index, jnp.maximum(place * block_count - 1, 0), 1),
        -1,
    )
    own_ids = lax.dynamic_slice_in_dim(segment_index, place * block_count, block_count)
    block_starts = (own_ids != jnp.concatenate([earlier_id, own_ids[:-1]])).astype(jnp.float32)
    keep_block = 1.0 - block_starts
    keep_token = jnp.concatenate(
        [keep_block[:, None], jnp.ones((block_count, BLK - 1), jnp.float32)], axis=1
    ).reshape(-1)
    x_input = block_input.astype(jnp.float32)
    norm_one, norm_one_pull = jax.vjp(layer_norm, x_input, chan_vals[0], chan_vals[1])
    edge_one = from_behind(norm_one[rows_here - 1 :], "seq", 1)
    shift_one = jnp.concatenate([edge_one, norm_one[:-1]], axis=0) * keep_token[:, None] - norm_one
    recv_in, decay_input, key_in, value_input, rate_input, gate_input = [
        (norm_one + shift_one * chan_vals[4 + number]).astype(jnp.bfloat16) for number in range(6)
    ]
    receptance_unscaled = product_matrix(recv_in, mix_full[0])
    key_unscaled = product_matrix(key_in, mix_full[1])
    value_unscaled = product_matrix(value_input, mix_full[2])
    decay_lowrank_output = product_matrix(decay_input, down_full[:, :first_boundary])
    rate_lowrank_output = product_matrix(rate_input, down_full[:, first_boundary:second_boundary])
    value_lowrank_output = product_matrix(value_input, down_full[:, second_boundary:third_boundary])
    gate_lowrank_output = product_matrix(gate_input, down_full[:, third_boundary:])
    decay_hidden = jnp.tanh(decay_lowrank_output).astype(jnp.bfloat16)
    rate_hidden = rate_lowrank_output.astype(jnp.bfloat16)
    value_hidden = value_lowrank_output.astype(jnp.bfloat16)
    gate_sig = jax.nn.sigmoid(gate_lowrank_output)
    gate_hid = gate_sig.astype(jnp.bfloat16)
    decay_low_rank = product_matrix(decay_hidden, upper_triangle_full[:first_boundary])
    rate_low_rank = product_matrix(rate_hidden, upper_triangle_full[first_boundary:second_boundary])
    value_low_rank = product_matrix(
        value_hidden, upper_triangle_full[second_boundary:third_boundary]
    )
    gate_activation = product_matrix(gate_hid, upper_triangle_full[third_boundary:])
    first_values = first_layer_value.astype(jnp.float32)
    prepared_inputs, prepare_pull = jax.vjp(
        prepare_inputs,
        receptance_unscaled,
        key_unscaled,
        value_unscaled,
        decay_low_rank,
        rate_low_rank,
        value_low_rank,
        first_values,
        attend_elements,
    )
    local_out, local_pull = jax.vjp(partial(recurrence, keep=keep_block), *prepared_inputs)
    unit_maps = jnp.broadcast_to(
        jnp.eye(ATTEND_DIM, dtype=jnp.float32), (attend_count, ATTEND_DIM, ATTEND_DIM)
    )
    zero_adds = jnp.zeros((attend_count, ATTEND_DIM, ATTEND_DIM), jnp.float32)
    chained = prefix((local_out[3], local_out[2]), "seq", compose, (unit_maps, zero_adds), False)
    start_state = chained[1]
    read_out = local_out[0] + jnp.einsum(
        "hij,thj->thi", start_state, local_out[1], precision=PRECISE
    )
    mixed_f, finish_pull = jax.vjp(
        finish,
        read_out,
        prepared_inputs[0],
        prepared_inputs[4],
        prepared_inputs[5],
        gate_activation,
        attend_elements,
    )
    mixed_low = mixed_f.astype(jnp.bfloat16)
    hidden_in = x_input + lax.psum(product_matrix(mixed_low, out_full), "head")
    norm_two, norm_two_pull = jax.vjp(layer_norm, hidden_in, chan_vals[2], chan_vals[3])
    edge_two = from_behind(norm_two[rows_here - 1 :], "seq", 1)
    shift_two = jnp.concatenate([edge_two, norm_two[:-1]], axis=0) * keep_token[:, None] - norm_two
    key_two = (norm_two + shift_two * chan_vals[10]).astype(jnp.bfloat16)
    pre_act = product_matrix(key_two, key_full)
    activated = jnp.square(jax.nn.relu(pre_act)).astype(jnp.bfloat16)
    block_out = hidden_in + lax.psum(product_matrix(activated, value_full), "head")
    grad_output = output_gradient.astype(jnp.float32)
    grad_ffo = grad_output.astype(jnp.bfloat16)
    grad_value2 = weight_grad(activated, grad_ffo)
    grad_pre = (back_product(grad_ffo, value_full) * 2.0 * jax.nn.relu(pre_act)).astype(
        jnp.bfloat16
    )
    grad_key2 = weight_grad(key_two, grad_pre)
    part_key_two = back_product(grad_pre, key_full)
    part_coeff_two = jnp.sum(part_key_two * shift_two, axis=0)
    grad_key_two, grad_coeff_two = lax.psum((part_key_two, part_coeff_two), "head")
    toward_two = grad_key_two * chan_vals[10] * keep_token[:, None]
    back_two = from_behind(toward_two[:1], "seq", -1)
    grad_norm_two = grad_key_two * (1.0 - chan_vals[10]) + jnp.concatenate(
        [toward_two[1:], back_two], axis=0
    )
    grad_hidden, grad_gain_two, grad_bias_two = norm_two_pull(grad_norm_two)
    grad_hidden = grad_hidden + grad_output
    grad_attn = grad_hidden.astype(jnp.bfloat16)
    grad_out_mat = weight_grad(mixed_low, grad_attn)
    grad_mixed = back_product(grad_attn, out_full)
    grad_read, grad_recv_a, grad_key_a, grad_value_a, grad_gate, grad_head_a = finish_pull(
        grad_mixed
    )
    local_carry = jnp.einsum("thi,thj->hij", grad_read, local_out[1], precision=PRECISE)
    backward = prefix(
        (jnp.swapaxes(local_out[3], 1, 2), local_carry),
        "seq",
        compose,
        (unit_maps, zero_adds),
        True,
    )
    grad_end = backward[1]
    grad_unit = jnp.einsum("thi,hij->thj", grad_read, start_state, precision=PRECISE)
    grad_map = jnp.einsum("hij,hik->hjk", start_state, grad_end, precision=PRECISE)
    chain_grads = local_pull((grad_read, grad_unit, grad_end, grad_map))
    cotangents = (
        grad_recv_a + chain_grads[0],
        chain_grads[1],
        chain_grads[2],
        chain_grads[3],
        grad_key_a + chain_grads[4],
        grad_value_a + chain_grads[5],
    )
    (
        grad_recv_raw,
        grad_key_raw,
        grad_value_raw,
        gradient_decay_low_rank,
        gradient_rate_low_rank,
        gradient_value_low_rank,
        grad_first,
        grad_head_b,
    ) = prepare_pull(cotangents)
    recv_round = grad_recv_raw.astype(jnp.bfloat16)
    key_round = grad_key_raw.astype(jnp.bfloat16)
    value_round = grad_value_raw.astype(jnp.bfloat16)
    decay_truncated = gradient_decay_low_rank.astype(jnp.bfloat16)
    rate_truncated = gradient_rate_low_rank.astype(jnp.bfloat16)
    value_low_rank_truncated = gradient_value_low_rank.astype(jnp.bfloat16)
    gate_round = grad_gate.astype(jnp.bfloat16)
    grad_mix = jnp.stack(
        [
            weight_grad(recv_in, recv_round),
            weight_grad(key_in, key_round),
            weight_grad(value_input, value_round),
        ]
    )
    grad_upper = jnp.concatenate(
        [
            weight_grad(decay_hidden, decay_truncated),
            weight_grad(rate_hidden, rate_truncated),
            weight_grad(value_hidden, value_low_rank_truncated),
            weight_grad(gate_hid, gate_round),
        ],
        axis=0,
    )
    part_hidden = jnp.concatenate(
        [
            back_product(decay_truncated, upper_triangle_full[:first_boundary]),
            back_product(rate_truncated, upper_triangle_full[first_boundary:second_boundary]),
            back_product(
                value_low_rank_truncated, upper_triangle_full[second_boundary:third_boundary]
            ),
            back_product(gate_round, upper_triangle_full[third_boundary:]),
        ],
        axis=1,
    )
    part_recv = back_product(recv_round, mix_full[0])
    part_key = back_product(key_round, mix_full[1])
    part_value = back_product(value_round, mix_full[2])
    hidden_sum, grad_recv_in, grad_key_in, grad_value_part = lax.psum(
        (part_hidden, part_recv, part_key, part_value), "head"
    )
    tanh_decay = jnp.tanh(decay_lowrank_output)
    decay_low_round = (hidden_sum[:, :first_boundary] * (1.0 - tanh_decay * tanh_decay)).astype(
        jnp.bfloat16
    )
    rate_low_round = hidden_sum[:, first_boundary:second_boundary].astype(jnp.bfloat16)
    value_low_round = hidden_sum[:, second_boundary:third_boundary].astype(jnp.bfloat16)
    gate_low_round = (hidden_sum[:, third_boundary:] * gate_sig * (1.0 - gate_sig)).astype(
        jnp.bfloat16
    )
    grad_down = jnp.concatenate(
        [
            weight_grad(decay_input, decay_low_round),
            weight_grad(rate_input, rate_low_round),
            weight_grad(value_input, value_low_round),
            weight_grad(gate_input, gate_low_round),
        ],
        axis=1,
    )
    grad_decay_in = back_product(decay_low_round, down_full[:, :first_boundary])
    grad_rate_in = back_product(rate_low_round, down_full[:, first_boundary:second_boundary])
    grad_value_in = grad_value_part + back_product(
        value_low_round, down_full[:, second_boundary:third_boundary]
    )
    grad_gate_in = back_product(gate_low_round, down_full[:, third_boundary:])
    mix_grads = (
        grad_recv_in,
        grad_decay_in,
        grad_key_in,
        grad_value_in,
        grad_rate_in,
        grad_gate_in,
    )
    grad_coeffs = jnp.stack([jnp.sum(gradient * shift_one, axis=0) for gradient in mix_grads])
    direct_one = mix_grads[0] * (1.0 - chan_vals[4])
    toward_one = mix_grads[0] * chan_vals[4]
    for number in range(1, 6):
        direct_one = direct_one + mix_grads[number] * (1.0 - chan_vals[4 + number])
        toward_one = toward_one + mix_grads[number] * chan_vals[4 + number]
    toward_one = toward_one * keep_token[:, None]
    back_one = from_behind(toward_one[:1], "seq", -1)
    grad_norm_one = direct_one + jnp.concatenate([toward_one[1:], back_one], axis=0)
    grad_input, grad_gain_one, grad_bias_one = norm_one_pull(grad_norm_one)
    grad_input = grad_input + grad_hidden
    grad_chan = jnp.concatenate(
        [
            jnp.stack([grad_gain_one, grad_bias_one, grad_gain_two, grad_bias_two]),
            grad_coeffs,
            grad_coeff_two[None],
        ],
        axis=0,
    )
    grad_head = grad_head_a + grad_head_b
    reduced = (
        lax.psum_scatter(grad_mix, "seq", scatter_dimension=1, tiled=True),
        lax.psum_scatter(grad_out_mat, "seq", scatter_dimension=1, tiled=True),
        lax.psum_scatter(grad_down, "seq", scatter_dimension=0, tiled=True),
        lax.psum_scatter(grad_upper, "seq", scatter_dimension=1, tiled=True),
        lax.psum_scatter(grad_key2, "seq", scatter_dimension=0, tiled=True),
        lax.psum_scatter(grad_value2, "seq", scatter_dimension=1, tiled=True),
        lax.psum_scatter(grad_head, "seq", scatter_dimension=1, tiled=True),
        lax.psum_scatter(grad_chan, "seq", scatter_dimension=1, tiled=True),
    )
    return (
        block_out.astype(jnp.bfloat16),
        grad_input,
        grad_first,
        reduced[7],
        reduced[6],
        reduced[0],
        reduced[1],
        reduced[2],
        reduced[3],
        reduced[4],
        reduced[5],
    )


def solution(mesh):
    in_specs = (
        P("seq", None),
        P("seq", "head"),
        P("seq", None),
        P(),
        P(None, "seq"),
        P(None, ("head", "seq")),
        P(None, "seq", "head"),
        P("head", "seq"),
        P("seq", None),
        P(None, ("head", "seq")),
        P("seq", "head"),
        P("head", "seq"),
    )
    out_specs = (
        P("seq", None),
        P("seq", None),
        P("seq", "head"),
        P(None, "seq"),
        P(None, ("head", "seq")),
        P(None, "seq", "head"),
        P("head", "seq"),
        P("seq", None),
        P(None, ("head", "seq")),
        P("seq", "head"),
        P("head", "seq"),
    )
    return jax.shard_map(shards, mesh=mesh, in_specs=in_specs, out_specs=out_specs, check_vma=False)
```

profile of v0, /device:TPU:0, one launch (start us, length us, event | category | flops | bytes accessed | tf_op | source)
XLA Modules:
  0.0 2414.9 jit_solution(13435228603012458156)
XLA Ops:
  8.0 43.2 %all-gather.5 = bf16[16,64,11]{1,2,0:T(8,128)(2,1)S(1)} all-gather(bf16[1,64,11]{1,2,0:T(8,128)(2,1)} %bitcast.1008), channel_id=1, replica_groups=mesh['seq'=16,'head'=2] {'seq'}, dimensions={0}, use_global_device_ids=true | all-gather | bytes 23936 | tf_op jit(solution)/shard_map/all_gather | solution.py:227
  58.7 36.6 %all-gather.4 = bf16[16,32,8]{1,2,0:T(8,128)(2,1)S(1)} all-gather(bf16[1,32,8]{1,2,0:T(8,128)(2,1)} %bitcast.1009), channel_id=1, replica_groups=mesh['seq'=16,'head'=2] {'seq'}, dimensions={0}, use_global_device_ids=true | all-gather | bytes 8704 | tf_op jit(solution)/shard_map/all_gather | solution.py:226
  96.1 39.8 %all_gather.51 = bf16[288,512]{0,1:T(8,128)(2,1)S(1)} all-gather(bf16[288,32]{0,1:T(8,128)(2,1)} %param.29), channel_id=1, replica_groups=mesh['seq'=16,'head'=2] {'seq'}, dimensions={1}, use_global_device_ids=true | all-gather | bytes 313344 | tf_op jit(solution)/shard_map/all_gather | solution.py:223
  137.2 40.8 %all_gather.50 = bf16[1024,288]{1,0:T(8,128)(2,1)S(1)} all-gather(bf16[64,288]{1,0:T(8,128)(2,1)} %param.28), channel_id=1, replica_groups=mesh['seq'=16,'head'=2] {'seq'}, dimensions={0}, use_global_device_ids=true | all-gather | bytes 626688 | tf_op jit(solution)/shard_map/all_gather | solution.py:222
  189.0 2.3 fusion.277
  192.5 2.3 multiply_add_fusion.5
  197.6 2.5 fusion.200
  200.9 174.3 %while.120 = (s32[]{:T(128)}, f32[8,128,64]{1,2,0:T(8,128)S(1)}, f32[8,8,16,128]{3,1,2,0:T(8,128)}, f32[8,8,16,64]{3,1,2,0:T(8,128)}, f32[8,8,16,64]{3,1,2,0:T(8...) while((s32[]{:T(128)}, f32[8,128,64]{1,2,0:T(8,128)S(1)}, ...), condition=%wide.region_5.6_spmd.clone.clone, body=%wide.region_3.5_spmd.clone.clone.sunk | while | flops 72363520 | bytes 7058341 | solution.py:186
  376.5 2.0 slice_bitcast_fusion.10
  384.4 67.3 %all-gather.23.cloned.1.call-done = f32[128,64,64]{2,1,0:T(8,128)} async-done(((f32[8,64,64]{2,1,0:T(8,128)}), f32[128,64,64]{2,1,0:T(8,128)}) %all-gather.23.cloned.1.call-update) | async-done | bytes 2097168 | tf_op jit(solution)/shard_map/all_gather | solution.py:28
  451.7 77.5 %all-gather.25.cloned.1.call-done = f32[128,64,64]{2,1,0:T(8,128)} async-done(((f32[8,64,64]{2,1,0:T(8,128)}), f32[128,64,64]{2,1,0:T(8,128)}) %all-gather.25.cloned.1.call-update) | async-done | bytes 2097168 | tf_op jit(solution)/shard_map/all_gather | solution.py:28
  531.8 2.0 multiply_convert_fusion.2
  533.8 51.9 %all-gather.17.cloned.1.call-done = bf16[512,1024]{0,1:T(8,128)(2,1)} async-done(((bf16[512,64]{0,1:T(8,128)(2,1)}), bf16[512,1024]{0,1:T(8,128)(2,1)}) %all-gather.17.cloned.1.call-update) | async-done | bytes 1048592 | tf_op jit(solution)/shard_map/all_gather | solution.py:221
  585.7 2.5 fusion.281
  589.6 16.4 all-reduce.21.cloned.1.call-done
  607.7 3.6 collective-permute-start.1
  613.6 72.7 %all-gather.19.cloned.1.call-done = bf16[1024,2048]{1,0:T(8,128)(2,1)} async-done(((bf16[64,2048]{1,0:T(8,128)(2,1)}), bf16[1024,2048]{1,0:T(8,128)(2,1)}) %all-gather.19.cloned.1.call-update) | async-done | bytes 4194320 | tf_op jit(solution)/shard_map/all_gather | solution.py:224
  686.3 3.0 convolution_maximum_fusion
  689.4 74.8 %all-gather.21.cloned.1.call-done = bf16[2048,1024]{0,1:T(8,128)(2,1)} async-done(((bf16[2048,64]{0,1:T(8,128)(2,1)}), bf16[2048,1024]{0,1:T(8,128)(2,1)}) %all-gather.21.cloned.1.call-update) | async-done | bytes 4194320 | tf_op jit(solution)/shard_map/all_gather | solution.py:225
  764.2 3.1 fusion.168
  768.1 2.3 fusion.282
  772.3 15.6 all-reduce.23.cloned.1.call-done
  790.6 4.2 collective-permute-done.2
  794.7 1.9 multiply_reduce_fusion.7
  803.4 2.2 fusion.283
  808.1 2.2 copy_bitcast_fusion.29
  810.3 4.6 fusion.222
  816.1 2.0 copy.391
  819.1 1.9 fusion.223
  821.0 46.9 %all-gather.27.cloned.1.call-done = f32[128,64,64]{2,1,0:T(8,128)} async-done(((f32[8,64,64]{2,1,0:T(8,128)}), f32[128,64,64]{2,1,0:T(8,128)}) %all-gather.27.cloned.1.call-update) | async-done | bytes 2097168 | tf_op jit(solution)/shard_map/all_gather | solution.py:28
  868.0 77.3 %all-gather.29.cloned.1.call-done = f32[128,64,64]{2,1,0:T(8,128)} async-done(((f32[8,64,64]{2,1,0:T(8,128)}), f32[128,64,64]{2,1,0:T(8,128)}) %all-gather.29.cloned.1.call-update) | async-done | bytes 2097168 | tf_op jit(solution)/shard_map/all_gather | solution.py:28
  945.3 40.8 %while.119 = (s32[]{:T(128)}, f32[8,64,64]{1,2,0:T(8,128)S(1)}, s32[]{:T(128)}, f32[16,8,64,64]{3,2,1,0:T(8,128)}, f32[16,8,64,64]{3,2,1,0:T(8,128)}, /*index=5*/s32[]{:T(128)}, s32[]{:T(128)}, s32[]{:T(128)}, s32[]{:T(128)}) while((s32[]{:T(128)}, f32[8,64,64]{1,2,0:T(8,128)S(1)}, s32[]{:T(128)}, f32[16,8,64,64]{3,2,1,0:T(8,128)}, ...), condition=%wide.region_22.23_spmd, body=%wide.region_21.22_spmd.sunk | while | flops 25198596 | bytes 1441947 | solution.py:37
  991.8 362.0 %while.121 = (s32[]{:T(128)}, f32[8,128,64]{1,2,0:T(8,128)S(1)}, f32[8,8,16,64]{3,2,1,0:T(8,128)}, f32[8,8,16,64]{3,2,1,0:T(8,128)}, f32[8,8,16,64]{3,2,1,0:T(8,...) while((s32[]{:T(128)}, f32[8,128,64]{1,2,0:T(8,128)S(1)}, ...), condition=%wide.region_27.28_spmd.clone.clone, body=%wide.region_23.27_spmd.clone.clone.sunk | while | flops 144026624 | bytes 10140189 | solution.py:186
  1353.9 2.0 copy.487
  1358.7 2.5 add_convert_fusion.8
  1369.0 1.8 copy.427
  1370.8 2.0 copy.415
  1372.8 1.9 reshape.432
  1374.7 2.0 copy.411
  1376.7 1.9 reshape.430
  1378.7 3.2 multiply_reduce_fusion.11
  1381.8 2.4 fusion.270
  1385.6 2.1 fusion.272
  1389.3 2.5 fusion.184
  1391.8 2.2 fusion.182
  1394.0 2.2 fusion.186
  1401.5 12.4 all-reduce.25.cloned.1.call-done
  1419.1 2.2 multiply_reduce_fusion.1
  1422.7 3.1 psum.63
  1427.5 2.9 fusion.264
  1434.6 2.8 fusion.285
  1442.4 2.2 copy.455
  1448.1 2.9 copy.453
  1451.1 4.6 fusion.286
  1456.7 4.6 fusion.221
  1463.6 3.3 pad_maximum_fusion
  1467.0 26.6 %reduce-scatter.27.cloned.1.call-done = f32[32,8]{1,0:T(8,128)} async-done(((f32[512,8]{1,0:T(8,128)}), f32[32,8]{1,0:T(8,128)}) %reduce-scatter.27.cloned.1.call-update) | async-done | bytes 1040
  1496.8 72.0 %reduce-scatter.25.cloned.1.call-done = f32[64,11]{1,0:T(8,128)} async-done(((f32[1024,11]{1,0:T(8,128)}), f32[64,11]{1,0:T(8,128)}) %reduce-scatter.25.cloned.1.call-update) | async-done | bytes 2832
  1570.2 78.3 %reduce-scatter.19.cloned.1.call-done = f32[512,64]{0,1:T(8,128)} async-done(((f32[512,1024]{0,1:T(8,128)}), f32[512,64]{0,1:T(8,128)}) %reduce-scatter.19.cloned.1.call-update) | async-done | bytes 131088 | tf_op jit(solution)/shard_map/reduce_scatter | solution.py:471
  1648.5 125.5 %reduce-scatter.31.cloned.1.call-done = f32[32,288]{1,0:T(8,128)} async-done(((f32[512,288]{1,0:T(8,128)}), f32[32,288]{1,0:T(8,128)}) %reduce-scatter.31.cloned.1.call-update) | async-done | bytes 36880
  1774.0 129.5 %reduce-scatter.29.cloned.1.call-done = f32[64,288]{1,0:T(8,128)} async-done(((f32[1024,288]{1,0:T(8,128)}), f32[64,288]{1,0:T(8,128)}) %reduce-scatter.29.cloned.1.call-update) | async-done | bytes 73744
  1903.5 179.7 %reduce-scatter.21.cloned.1.call-done = f32[64,2048]{1,0:T(8,128)} async-done(((f32[1024,2048]{1,0:T(8,128)}), f32[64,2048]{1,0:T(8,128)}) %reduce-scatter.21.cloned.1.call-update) | async-done | bytes 524304 | tf_op jit(solution)/shard_map/reduce_scatter | solution.py:474
  2083.2 183.1 %reduce-scatter.23.cloned.1.call-done = f32[2048,64]{0,1:T(8,128)} async-done(((f32[2048,1024]{0,1:T(8,128)}), f32[2048,64]{0,1:T(8,128)}) %reduce-scatter.23.cloned.1.call-update) | async-done | bytes 524304 | tf_op jit(solution)/shard_map/reduce_scatter | solution.py:475
  2266.3 141.6 %reduce-scatter.17.cloned.1.call-done = f32[3,64,512]{2,1,0:T(8,128)} async-done(((f32[3,1024,512]{2,1,0:T(8,128)}), f32[3,64,512]{2,1,0:T(8,128)}) %reduce-scatter.17.cloned.1.call-update) | async-done | bytes 393232 | tf_op jit(solution)/shard_map/reduce_scatter | solution.py:470
  (1202 shorter events, 683.1 us)
Async XLA Ops:
  7.2 171.8 %copy-start = (bf16[128,1024]{1,0:T(8,128)(2,1)S(1)}, bf16[128,1024]{1,0:T(8,128)(2,1)}, u32[]{:S(2)}) copy-start(bf16[128,1024]{1,0:T(8,128)(2,1)} %param.20) | copy-start | bytes 786436
  7.2 170.8 %copy-start.130 = (s32[128]{0:T(128)S(1)}, s32[128]{0:T(128)}, u32[]{:S(2)}) copy-start(s32[128]{0:T(128)} %param.23) | copy-start | bytes 1540
  7.2 179.4 %all-gather.15.cloned.1.call-start = ((), (), s32[]{:S(2)}) async-start(), calls=%async_computation.8 | async-start | bytes 3342336 | tf_op jit(solution)/shard_map/all_gather | solution.py:220
  7.9 443.8 %all-gather.23.cloned.1.call-start = ((), (), s32[]{:S(2)}) async-start(), calls=%async_computation.18 | async-start | bytes 4456448 | tf_op jit(solution)/shard_map/all_gather | solution.py:28
  52.3 129.7 %copy-start.103 = (f32[128]{0:T(128)}, f32[128]{0:T(128)S(1)}, u32[]{:S(2)}) copy-start(f32[128]{0:T(128)S(1)} %broadcast_multiply_fusion.3) | copy-start | bytes 1540
  53.5 128.5 %copy-start.113 = (f32[128]{0:T(128)}, f32[128]{0:T(128)S(1)}, u32[]{:S(2)}) copy-start(f32[128]{0:T(128)S(1)} %fusion.261) | copy-start | bytes 1540
  54.2 127.8 %copy-start.83 = (f32[1,1024]{1,0:T(1,128)}, f32[1,1024]{1,0:T(1,128)S(1)}, u32[]{:S(2)}) copy-start(f32[1,1024]{1,0:T(1,128)S(1)} %get-tuple-element.2240) | copy-start | bytes 12292
  54.2 127.8 %copy-start.85 = (f32[1,1024]{1,0:T(1,128)}, f32[1,1024]{1,0:T(1,128)S(1)}, u32[]{:S(2)}) copy-start(f32[1,1024]{1,0:T(1,128)S(1)} %get-tuple-element.2241) | copy-start | bytes 12292
  54.2 127.8 %copy-start.87 = (f32[1,1024]{1,0:T(1,128)}, f32[1,1024]{1,0:T(1,128)S(1)}, u32[]{:S(2)}) copy-start(f32[1,1024]{1,0:T(1,128)S(1)} %get-tuple-element.2242) | copy-start | bytes 12292
  54.2 127.8 %copy-start.89 = (f32[1,1024]{1,0:T(1,128)}, f32[1,1024]{1,0:T(1,128)S(1)}, u32[]{:S(2)}) copy-start(f32[1,1024]{1,0:T(1,128)S(1)} %get-tuple-element.2243) | copy-start | bytes 12292
  54.2 127.8 %copy-start.91 = (f32[1,1024]{1,0:T(1,128)}, f32[1,1024]{1,0:T(1,128)S(1)}, u32[]{:S(2)}) copy-start(f32[1,1024]{1,0:T(1,128)S(1)} %get-tuple-element.2244) | copy-start | bytes 12292
  54.2 127.8 %copy-start.93 = (f32[1,1024]{1,0:T(1,128)}, f32[1,1024]{1,0:T(1,128)S(1)}, u32[]{:S(2)}) copy-start(f32[1,1024]{1,0:T(1,128)S(1)} %get-tuple-element.2245) | copy-start | bytes 12292
  55.5 123.5 %collective-permute-start = (f32[1,1024]{1,0:T(1,128)S(1)}, f32[1,1024]{1,0:T(1,128)S(1)}, u32[]{:S(2)}, u32[]{:S(2)}) collective-permute-start(f32[1,1024]{1,0:T(1,128)S(1)} %slice.224), channel_id=1, source_target_pairs={{0,2},{2,4},{4,6},{6,8},{8,10},{10,12},{12,14},{14,16},{16,18},{18... | collective-permute-start | bytes 12296 | tf_op jit(solution)/shard_map/ppermute | solution.py:21
  135.9 50.3 %copy-start.31 = (bf16[288,512]{0,1:T(8,128)(2,1)}, bf16[288,512]{0,1:T(8,128)(2,1)S(1)}, u32[]{:S(2)}) copy-start(bf16[288,512]{0,1:T(8,128)(2,1)S(1)} %all_gather.51) | copy-start | bytes 884740
  177.9 202.2 %copy-start.3 = (bf16[1024,288]{1,0:T(8,128)(2,1)}, bf16[1024,288]{1,0:T(8,128)(2,1)S(1)}, u32[]{:S(2)}) copy-start(bf16[1024,288]{1,0:T(8,128)(2,1)S(1)} %all_gather.50) | copy-start | bytes 1769476
  200.9 178.9 %copy-start.119 = (f32[512]{0:T(512)S(1)}, f32[512]{0:T(512)}, u32[]{:S(2)}) copy-start(f32[512]{0:T(512)} %get-tuple-element.1938) | copy-start | bytes 6148
  200.9 179.0 %copy-start.118 = (f32[512]{0:T(512)S(1)}, f32[512]{0:T(512)}, u32[]{:S(2)}) copy-start(f32[512]{0:T(512)} %get-tuple-element.1939) | copy-start | bytes 6148
  200.9 179.1 %copy-start.117 = (f32[512]{0:T(512)S(1)}, f32[512]{0:T(512)}, u32[]{:S(2)}) copy-start(f32[512]{0:T(512)} %get-tuple-element.1937) | copy-start | bytes 6148
  378.5 150.7 %all-gather.25.cloned.1.call-start = ((), (), s32[]{:S(2)}) async-start(), calls=%async_computation.19 | async-start | bytes 4456448 | tf_op jit(solution)/shard_map/all_gather | solution.py:28
  379.2 206.5 %all-gather.17.cloned.1.call-start = ((), (), s32[]{:S(2)}) async-start(), calls=%async_computation.9 | async-start | bytes 1114112 | tf_op jit(solution)/shard_map/all_gather | solution.py:221
  379.8 226.2 %all-reduce.21.cloned.1.call-start = ((), (), s32[]{:S(2)}) async-start(), calls=%async_computation.10 | async-start | bytes 1048576 | tf_op jit(solution)/shard_map/psum | solution.py:316
  381.5 150.3 %copy-start.68 = (f32[128,128]{0,1:T(8,128)}, f32[128,128]{0,1:T(8,128)S(1)}, u32[]{:S(2)}) copy-start(f32[128,128]{0,1:T(8,128)S(1)} %fusion.181) | copy-start | bytes 196612
  384.0 145.4 %copy-start.38 = (f32[128,8,64]{0,2,1:T(8,128)}, f32[128,8,64]{0,2,1:T(8,128)S(1)}, u32[]{:S(2)}) copy-start(f32[128,8,64]{0,2,1:T(8,128)S(1)} %copy.486) | copy-start | bytes 786436
  384.3 146.5 %copy-start.81 = (f32[128,8]{0,1:T(8,128)}, f32[128,8]{0,1:T(8,128)S(1)}, u32[]{:S(2)}) copy-start(f32[128,8]{0,1:T(8,128)S(1)} %multiply_reduce_fusion.17) | copy-start | bytes 12292
  531.4 76.0 %copy-start.78 = (f32[128,8]{0,1:T(8,128)}, f32[128,8]{0,1:T(8,128)S(1)}, u32[]{:S(2)}) copy-start(f32[128,8]{0,1:T(8,128)S(1)} %fusion.259) | copy-start | bytes 12292
  531.6 75.8 %copy-start.96 = (f32[1,1024]{1,0:T(1,128)S(1)}, f32[1,1024]{1,0:T(1,128)}, u32[]{:S(2)}) copy-start(f32[1,1024]{1,0:T(1,128)} %get-tuple-element.2238) | copy-start | bytes 12292
  531.8 75.8 %copy-start.39 = (f32[128,512]{1,0:T(8,128)}, f32[128,512]{1,0:T(8,128)S(1)}, u32[]{:S(2)}) copy-start(f32[128,512]{1,0:T(8,128)S(1)} %copy.384) | copy-start | bytes 786436
  531.8 80.8 %copy-start.95 = (f32[1,1024]{1,0:T(1,128)S(1)}, f32[1,1024]{1,0:T(1,128)}, u32[]{:S(2)}) copy-start(f32[1,1024]{1,0:T(1,128)} %get-tuple-element.2237) | copy-start | bytes 12292
  531.8 80.8 %copy-start.111 = (f32[128]{0:T(128)S(1)}, f32[128]{0:T(128)}, u32[]{:S(2)}) copy-start(f32[128]{0:T(128)} %copy-done.110) | copy-start | bytes 1540
  533.8 55.8 %copy-start.59 = (bf16[128,512]{1,0:T(8,128)(2,1)}, bf16[128,512]{1,0:T(8,128)(2,1)S(1)}, u32[]{:S(2)}) copy-start(bf16[128,512]{1,0:T(8,128)(2,1)S(1)} %get-tuple-element.2262) | copy-start | bytes 393220
  588.2 98.1 %all-gather.19.cloned.1.call-start = ((), (), s32[]{:S(2)}) async-start(), calls=%async_computation.11 | async-start | bytes 4456448 | tf_op jit(solution)/shard_map/all_gather | solution.py:224
  588.8 175.4 %all-gather.21.cloned.1.call-start = ((), (), s32[]{:S(2)}) async-start(), calls=%async_computation.12 | async-start | bytes 4456448 | tf_op jit(solution)/shard_map/all_gather | solution.py:225
  589.6 198.3 %all-reduce.23.cloned.1.call-start = ((), (), s32[]{:S(2)}) async-start(), calls=%async_computation.13 | async-start | bytes 1048576 | tf_op jit(solution)/shard_map/psum | solution.py:333
  607.7 5.0 collective-permute-start.1
  612.6 76.7 %copy-start.107 = (f32[1,1024]{1,0:T(1,128)}, f32[1,1024]{1,0:T(1,128)S(1)}, u32[]{:S(2)}) copy-start(f32[1,1024]{1,0:T(1,128)S(1)} %collective-permute-done.1) | copy-start | bytes 12292
  612.6 151.6 %copy-start.29 = (bf16[128,1024]{1,0:T(8,128)(2,1)S(1)}, bf16[128,1024]{1,0:T(8,128)(2,1)}, u32[]{:S(2)}) copy-start(bf16[128,1024]{1,0:T(8,128)(2,1)} %param.22) | copy-start | bytes 786436
  768.1 26.6 %copy-start.109 = (f32[1,1024]{1,0:T(1,128)S(1)}, f32[1,1024]{1,0:T(1,128)}, u32[]{:S(2)}) copy-start(f32[1,1024]{1,0:T(1,128)} %get-tuple-element.2236) | copy-start | bytes 12292
  770.4 97.6 %all-gather.27.cloned.1.call-start = ((), (), s32[]{:S(2)}) async-start(), calls=%async_computation.20 | async-start | bytes 4456448 | tf_op jit(solution)/shard_map/all_gather | solution.py:28
  772.3 173.0 %all-gather.29.cloned.1.call-start = ((), (), s32[]{:S(2)}) async-start(), calls=%async_computation.21 | async-start | bytes 4456448 | tf_op jit(solution)/shard_map/all_gather | solution.py:28
  789.1 5.6 collective-permute-start.2
  805.6 608.3 %all-reduce.25.cloned.1.call-start = ((), (), s32[]{:S(2)}) async-start(), calls=%async_computation.26 | async-start | bytes 4489216 | tf_op jit(solution)/shard_map/psum | solution.py:323
  991.8 364.1 %copy-start.82 = (f32[128,8]{0,1:T(8,128)S(1)}, f32[128,8]{0,1:T(8,128)}, u32[]{:S(2)}) copy-start(f32[128,8]{0,1:T(8,128)} %copy-done.81) | copy-start | bytes 12292
  1366.0 12.6 copy-start.9
  1366.0 12.6 copy-start.116
  1391.7 25.0 %copy-start.4 = (bf16[1024,288]{1,0:T(8,128)(2,1)S(1)}, bf16[1024,288]{1,0:T(8,128)(2,1)}, u32[]{:S(2)}) copy-start(bf16[1024,288]{1,0:T(8,128)(2,1)} %copy-done.3) | copy-start | bytes 1769476
  1396.2 22.8 copy-start.7
  1396.2 22.8 copy-start.84
  1396.2 22.8 copy-start.86
  1396.2 22.8 copy-start.88
  1396.2 97.3 %reduce-scatter.27.cloned.1.call-start = ((), (), s32[]{:S(2)}) async-start(), calls=%async_computation.23 | async-start | bytes 278528
  1401.2 167.5 %reduce-scatter.25.cloned.1.call-start = ((), (), s32[]{:S(2)}) async-start(), calls=%async_computation.22 | async-start | bytes 557056
  1421.4 5.5 collective-permute-start.3
  1434.5 214.0 %reduce-scatter.19.cloned.1.call-start = ((), (), s32[]{:S(2)}) async-start(), calls=%async_computation.15 | async-start | bytes 2228224 | tf_op jit(solution)/shard_map/reduce_scatter | solution.py:471
  1437.4 336.7 %reduce-scatter.31.cloned.1.call-start = ((), (), s32[]{:S(2)}) async-start(), calls=%async_computation.25 | async-start | bytes 835584
  1444.7 458.9 %reduce-scatter.29.cloned.1.call-start = ((), (), s32[]{:S(2)}) async-start(), calls=%async_computation.24 | async-start | bytes 1671168
  1451.0 632.2 %reduce-scatter.21.cloned.1.call-start = ((), (), s32[]{:S(2)}) async-start(), calls=%async_computation.16 | async-start | bytes 8912896 | tf_op jit(solution)/shard_map/reduce_scatter | solution.py:474
  1455.7 810.6 %reduce-scatter.23.cloned.1.call-start = ((), (), s32[]{:S(2)}) async-start(), calls=%async_computation.17 | async-start | bytes 8912896 | tf_op jit(solution)/shard_map/reduce_scatter | solution.py:475
  1461.3 946.6 %reduce-scatter.17.cloned.1.call-start = ((), (), s32[]{:S(2)}) async-start(), calls=%async_computation.14 | async-start | bytes 6684672 | tf_op jit(solution)/shard_map/reduce_scatter | solution.py:470
  1466.9 28.0 %copy-start.69 = (f32[128,1024]{1,0:T(8,128)S(1)}, f32[128,1024]{1,0:T(8,128)}, u32[]{:S(2)}) copy-start(f32[128,1024]{1,0:T(8,128)} %get-tuple-element.2110) | copy-start | bytes 1572868
  1466.9 28.8 %copy-start.129 = (f32[128]{0:T(128)S(1)}, f32[128]{0:T(128)}, u32[]{:S(2)}) copy-start(f32[128]{0:T(128)} %get-tuple-element.1923) | copy-start | bytes 1540
  1466.9 28.8 %copy-start.19 = (f32[128,1024]{1,0:T(8,128)S(1)}, f32[128,1024]{1,0:T(8,128)}, u32[]{:S(2)}) copy-start(f32[128,1024]{1,0:T(8,128)} %copy-done.18) | copy-start | bytes 1572868
  1466.9 28.8 %copy-start.115 = (f32[128]{0:T(128)S(1)}, f32[128]{0:T(128)}, u32[]{:S(2)}) copy-start(f32[128]{0:T(128)} %copy-done.113) | copy-start | bytes 1540
  1466.9 28.8 %copy-start.125 = (f32[128]{0:T(128)S(1)}, f32[128]{0:T(128)}, u32[]{:S(2)}) copy-start(f32[128]{0:T(128)} %copy-done.124) | copy-start | bytes 1540
  1466.9 28.8 %copy-start.127 = (f32[128]{0:T(128)S(1)}, f32[128]{0:T(128)}, u32[]{:S(2)}) copy-start(f32[128]{0:T(128)} %copy-done.126) | copy-start | bytes 1540
  (90 other events, 453.4 us)
Sparse Core Ops, SparseCore 0:
  10.8 71.5 all-gather.14
  378.6 73.0 all-gather.22
  454.5 74.6 all-gather.24
  531.8 53.8 all-gather.16
  588.5 17.5 all-reduce.20
  609.0 77.2 all-gather.18
  689.5 74.6 all-gather.20
  770.5 17.3 all-reduce.22
  790.7 77.2 all-gather.26
  870.6 74.6 all-gather.28
  1396.3 17.5 all-reduce.24
  1416.1 77.3 reduce-scatter.26
  1495.8 72.9 reduce-scatter.24
  1571.6 76.9 reduce-scatter.18
  1654.3 119.6 reduce-scatter.30
  1780.0 123.5 reduce-scatter.28
  1906.4 176.8 reduce-scatter.20
  2086.1 180.2 reduce-scatter.22
  2269.3 138.5 reduce-scatter.16
where the time goes:
time: 2440 us; the launch traced here: 2410 us
  waiting for transfers between devices  1460 us (60%)
  matrix products  470 us (19%)
  local copies, waits for them, and re-layouts  175 us (7%)
  blocking collectives  163 us (7%)
  other arithmetic  118 us (5%)
    unnamed x23, waiting for transfers between devices  357 us
    all_gather x4, waiting for transfers between devices, prefix(): gathered = jax.tree.map(lambda a: lax.all_gather(a, axis), part)  269 us
    reduce_scatter x1, waiting for transfers between devices, shards(): lax.psum_scatter(grad_value2, 'seq', scatter_dimension=1, tiled=True)  183 us
    reduce_scatter x1, waiting for transfers between devices, shards(): lax.psum_scatter(grad_key2, 'seq', scatter_dimension=0, tiled=True)  180 us
    reduce_scatter x1, waiting for transfers between devices, shards(): lax.psum_scatter(grad_mix, 'seq', scatter_dimension=1, tiled=True)  142 us
    reduce_scatter x1, waiting for transfers between devices, shards(): lax.psum_scatter(grad_out_mat, 'seq', scatter_dimension=1, tiled=True)  78.3 us
    all_gather x1, waiting for transfers between devices, shards(): lax.all_gather(channel_value_matrix, 'seq', axis=1, tiled=True)  74.8 us
    all_gather x1, waiting for transfers between devices, shards(): lax.all_gather(channel_key_matrix, 'seq', axis=0, tiled=True)  72.7 us
  transfers between devices with their start and end apart: 23, of which 21 were waited for; matrix products, arithmetic and copies ran while one was open for 5% of the time, Pallas kernels for 0%

commit v1 on v0

v1 whole, which is shorter than its diff:
```python
from functools import partial

import jax
import jax.numpy as jnp
from jax import lax
from jax.sharding import PartitionSpec as P

ATTEND_DIM = 64
DECAY_LOW_RANK = 64
RATE_RANK = 64
VALUE_RANK = 32
BLK = 16


PRECISE = lax.Precision.HIGHEST
FINE = lax.Precision.HIGH


def from_behind(value, axis, steps):
    count = lax.axis_size(axis)
    initial, last = (max(0, -steps), min(count, count - steps))
    return lax.ppermute(value, axis, [(source, source + steps) for source in range(initial, last)])


def swap_sum(value):
    return value + lax.ppermute(value, "head", [(0, 1), (1, 0)])


def times(left, right, turned=False):
    shape = "hij,hkj->hik" if turned else "hij,hjk->hik"
    return jnp.einsum(shape, left, right, precision=FINE)


def chain_steps(count):
    return [1 << power for power in range((count - 1).bit_length())]


def exclusive_maps(own_map, direction):
    count = lax.axis_size("seq")
    place = lax.axis_index("seq")
    behind = place if direction > 0 else count - 1 - place
    maps = []
    total = own_map
    for step in chain_steps(count):
        maps.append(total)
        if 2 * step < count:
            arrived = from_behind(total, "seq", direction * step)
            total = jnp.where(behind >= step, times(arrived, total), total)
    return maps


def exclusive_chain(maps, own_add, direction):
    total = own_add
    for step, step_map in zip(chain_steps(lax.axis_size("seq")), maps):
        arrived = from_behind(total, "seq", direction * step)
        total = total + times(arrived, step_map)
    return from_behind(total, "seq", direction)


def halve_sum(rows, sent_type, order):
    count = lax.axis_size("seq")
    place = lax.axis_index("seq")
    bits = (count - 1).bit_length()
    left = list(range(bits - 1, -1, -1))
    held = rows.reshape((2,) * bits + (rows.shape[0] // count, rows.shape[1]))
    for bit in [number for number in order if number < bits] + list(range(len(order), bits)):
        where = left.index(bit)
        left.remove(bit)
        mine = (place >> bit) & 1
        kept = lax.dynamic_index_in_dim(held, mine, where, False)
        sent = lax.dynamic_index_in_dim(held, 1 - mine, where, False).astype(sent_type)
        pairs = [(number, number ^ (1 << bit)) for number in range(count)]
        held = kept.astype(jnp.float32) + lax.ppermute(sent, "seq", pairs).astype(jnp.float32)
    return held


def halves_side_by_side(rows, width):
    columns = rows.shape[1] // 2
    cut = rows.reshape(-1, width, 2 * columns)
    return jnp.concatenate([cut[:, :, :columns], cut[:, :, columns:]], axis=1).reshape(-1, columns)


def halves_stacked(rows, width):
    columns = rows.shape[1]
    cut = rows.reshape(-1, 2 * width, columns)
    return jnp.concatenate([cut[:, :width], cut[:, width:]], axis=2).reshape(-1, 2 * columns)


def product_matrix(operand, weights):
    return jnp.dot(operand, weights, preferred_element_type=jnp.float32)


def back_product(gradient, weights):
    return lax.dot_general(
        gradient, weights, (((1,), (1,)), ((), ())), preferred_element_type=jnp.float32
    )


def weight_grad(operand, gradient):
    return lax.dot_general(
        operand, gradient, (((0,), (0,)), ((), ())), preferred_element_type=jnp.float32
    )


def layer_norm(value_rows, scale_vec, offset_vec):
    centre = value_rows - jnp.mean(value_rows, axis=-1, keepdims=True)
    spread = jnp.mean(centre * centre, axis=-1, keepdims=True)
    return centre * lax.rsqrt(spread + 1e-05) * scale_vec + offset_vec


def prepare_inputs(
    receptance_unscaled,
    key_unscaled,
    value_unscaled,
    decay_low_rank,
    rate_low_rank,
    value_low_rank,
    first_layer_value,
    attend_elements,
):
    rows_here = receptance_unscaled.shape[0]
    attend_count = receptance_unscaled.shape[1] // ATTEND_DIM
    logarithm_scale = -jax.nn.softplus(-(attend_elements[0] + decay_low_rank)) - 0.5
    log_decay = -jnp.exp(logarithm_scale)
    rate_sigmoid = jax.nn.sigmoid(attend_elements[1] + rate_low_rank)
    payload_blended = value_unscaled + (first_layer_value - value_unscaled) * jax.nn.sigmoid(
        attend_elements[2] + value_low_rank
    )
    scaled = (key_unscaled * attend_elements[3]).reshape(rows_here, attend_count, ATTEND_DIM)
    unit_key = scaled * lax.rsqrt(jnp.sum(scaled * scaled, axis=-1, keepdims=True) + 1e-05)
    lookup_used = key_unscaled * (1.0 + (rate_sigmoid - 1.0) * attend_elements[4])
    layout = (rows_here, attend_count, ATTEND_DIM)
    return (
        receptance_unscaled.reshape(layout),
        log_decay.reshape(layout),
        -unit_key,
        unit_key * rate_sigmoid.reshape(layout),
        lookup_used.reshape(layout),
        payload_blended.reshape(layout),
    )


def finish(
    read_out, reader_vectors, lookup_used, payload_blended, gate_activation, attend_elements
):
    rows_here, attend_count, _ = read_out.shape
    centre = read_out - jnp.mean(read_out, axis=-1, keepdims=True)
    unit_length_vectors = centre * lax.rsqrt(
        jnp.mean(centre * centre, axis=-1, keepdims=True) + 0.00064
    )
    extra_addend = (
        jnp.sum(
            reader_vectors * lookup_used * attend_elements[5].reshape(attend_count, ATTEND_DIM),
            axis=-1,
            keepdims=True,
        )
        * payload_blended
    )
    final_answer = (
        unit_length_vectors * attend_elements[6].reshape(attend_count, ATTEND_DIM)
        + attend_elements[7].reshape(attend_count, ATTEND_DIM)
        + extra_addend
    )
    return final_answer.reshape(rows_here, attend_count * ATTEND_DIM) * gate_activation


@jax.custom_vjp
def unit_inverse(strict_part):
    unit = jnp.eye(strict_part.shape[-1], dtype=jnp.float32)[None]
    inverse = unit + strict_part
    power = strict_part
    for _ in range(BLK.bit_length() - 2):
        power = times(power, power)
        inverse = inverse + times(inverse, power)
    return inverse


def unit_inverse_keep(strict_part):
    inverse = unit_inverse(strict_part)
    return inverse, inverse


def unit_inverse_pull(inverse, gradient):
    turned = jnp.swapaxes(inverse, 1, 2)
    return (times(times(turned, gradient), turned),)


unit_inverse.defvjp(unit_inverse_keep, unit_inverse_pull)


def chunk_terms(reader_vectors, log_decay, removal, refill, lookup_used, payload_blended, keep):
    rows_here, attend_count, head_width = reader_vectors.shape
    block_count = rows_here // BLK
    recv, decay, removal, refill, lookup, payload = [
        jnp.transpose(rows, (1, 0, 2))
        for rows in (reader_vectors, log_decay, removal, refill, lookup_used, payload_blended)
    ]
    token = jnp.arange(rows_here)
    same = (token[:, None] // BLK) == (token[None, :] // BLK)
    strict = (same & (token[:, None] > token[None, :])).astype(jnp.float32)
    inclusive = (same & (token[:, None] >= token[None, :])).astype(jnp.float32)

    def blocks(rows):
        return rows.reshape(attend_count, block_count, BLK, head_width)

    cumulative = jnp.einsum("ts,hsj->htj", inclusive, decay, precision=PRECISE)
    growth = jnp.exp(-cumulative)
    refill_grown = refill * growth
    key_grown = lookup * growth
    first_term = removal * jnp.exp(cumulative - decay)
    reader_term = recv * jnp.exp(cumulative)
    mix_refill = times(first_term, refill_grown, True) * strict
    mix_key = times(first_term, key_grown, True) * strict
    read_refill = times(reader_term, refill_grown, True) * inclusive
    read_key = times(reader_term, key_grown, True) * inclusive
    inverse = unit_inverse(mix_refill)
    removed_map = times(inverse, first_term)
    removed_add = times(inverse, times(mix_key, payload))
    read_map = reader_term + times(read_refill, removed_map)
    read_add = times(read_refill, removed_add) + times(read_key, payload)
    total = blocks(cumulative)[:, :, BLK - 1 :]
    tail = jnp.exp(total - blocks(cumulative))
    refill_tail = blocks(refill) * tail
    key_tail = blocks(lookup) * tail

    def outer(left, right):
        return jnp.einsum("hcti,hctj->chij", blocks(left), right, precision=FINE)

    unit = jnp.eye(head_width, dtype=jnp.float32)
    kept = keep[:, None, None, None]
    decayed = jnp.exp(jnp.transpose(total, (1, 0, 2, 3)))
    state_map = (unit * decayed + outer(removed_map, refill_tail)) * kept
    state_add = outer(removed_add, refill_tail) + outer(payload, key_tail)
    return state_map, state_add, blocks(read_map) * keep[None, :, None, None], read_add


def shards(
    block_input,
    first_layer_value,
    output_gradient,
    segment_index,
    channel_parameters,
    head_parameters,
    mixing_weights,
    output_weight,
    low_rank_down_weight,
    low_rank_up_weight,
    channel_key_matrix,
    channel_value_matrix,
):
    width = low_rank_down_weight.shape[0]
    half = low_rank_up_weight.shape[1]
    hidden_local = mixing_weights.shape[2]
    low_columns = low_rank_down_weight.shape[1]
    head_rows = head_parameters.shape[0]
    own_columns = jnp.concatenate([low_rank_up_weight, head_parameters], axis=0).T
    first_pack = jnp.concatenate(
        [
            mixing_weights[0],
            mixing_weights[1],
            mixing_weights[2],
            low_rank_down_weight,
            halves_side_by_side(own_columns, half),
            channel_parameters.T,
        ],
        axis=1,
    )
    first_full = lax.all_gather(first_pack, "seq", axis=0, tiled=True)
    later_pack = jnp.concatenate(
        [output_weight.T, channel_key_matrix, channel_value_matrix.T], axis=1
    )
    later_full = lax.all_gather(later_pack, "seq", axis=0, tiled=True)
    mix_full = [
        first_full[:, number * hidden_local : (number + 1) * hidden_local] for number in range(3)
    ]
    place_down = 3 * hidden_local
    place_up = place_down + low_columns
    place_chan = place_up + (low_columns + head_rows) // 2
    down_full = first_full[:, place_down:place_up]
    columns_full = halves_stacked(first_full[:, place_up:place_chan], half)
    up_turned = columns_full[:, :low_columns]
    head_full = columns_full[:, low_columns:].T
    chan_full = first_full[:, place_chan:].T
    units = channel_key_matrix.shape[1]
    out_turned = later_full[:, :hidden_local]
    key_full = later_full[:, hidden_local : hidden_local + units]
    value_turned = later_full[:, hidden_local + units :]
    chan_vals = chan_full.astype(jnp.float32)
    attend_elements = head_full.astype(jnp.float32)
    first_boundary = DECAY_LOW_RANK
    second_boundary = first_boundary + RATE_RANK
    third_boundary = second_boundary + VALUE_RANK
    rows_here = block_input.shape[0]
    attend_count = head_full.shape[1] // ATTEND_DIM
    block_count = rows_here // BLK
    place = lax.axis_index("seq")
    earlier_id = jnp.where(
        place > 0,
        lax.dynamic_slice_in_dim(segment_index, jnp.maximum(place * block_count - 1, 0), 1),
        -1,
    )
    own_ids = lax.dynamic_slice_in_dim(segment_index, place * block_count, block_count)
    block_starts = (own_ids != jnp.concatenate([earlier_id, own_ids[:-1]])).astype(jnp.float32)
    keep_block = 1.0 - block_starts
    keep_token = jnp.concatenate(
        [keep_block[:, None], jnp.ones((block_count, BLK - 1), jnp.float32)], axis=1
    ).reshape(-1)
    x_input = block_input.astype(jnp.float32)
    norm_one, norm_one_pull = jax.vjp(layer_norm, x_input, chan_vals[0], chan_vals[1])
    edge_one = from_behind(norm_one[rows_here - 1 :], "seq", 1)
    shift_one = jnp.concatenate([edge_one, norm_one[:-1]], axis=0) * keep_token[:, None] - norm_one
    recv_in, decay_input, key_in, value_input, rate_input, gate_input = [
        (norm_one + shift_one * chan_vals[4 + number]).astype(jnp.bfloat16) for number in range(6)
    ]
    receptance_unscaled = product_matrix(recv_in, mix_full[0])
    key_unscaled = product_matrix(key_in, mix_full[1])
    value_unscaled = product_matrix(value_input, mix_full[2])
    decay_lowrank_output = product_matrix(decay_input, down_full[:, :first_boundary])
    rate_lowrank_output = product_matrix(rate_input, down_full[:, first_boundary:second_boundary])
    value_lowrank_output = product_matrix(value_input, down_full[:, second_boundary:third_boundary])
    gate_lowrank_output = product_matrix(gate_input, down_full[:, third_boundary:])
    decay_hidden = jnp.tanh(decay_lowrank_output).astype(jnp.bfloat16)
    rate_hidden = rate_lowrank_output.astype(jnp.bfloat16)
    value_hidden = value_lowrank_output.astype(jnp.bfloat16)
    gate_sig = jax.nn.sigmoid(gate_lowrank_output)
    gate_hid = gate_sig.astype(jnp.bfloat16)
    decay_low_rank = back_product(decay_hidden, up_turned[:, :first_boundary])
    rate_low_rank = back_product(rate_hidden, up_turned[:, first_boundary:second_boundary])
    value_low_rank = back_product(
        value_hidden, up_turned[:, second_boundary:third_boundary]
    )
    gate_activation = back_product(gate_hid, up_turned[:, third_boundary:])
    first_values = first_layer_value.astype(jnp.float32)
    prepared_inputs, prepare_pull = jax.vjp(
        prepare_inputs,
        receptance_unscaled,
        key_unscaled,
        value_unscaled,
        decay_low_rank,
        rate_low_rank,
        value_low_rank,
        first_values,
        attend_elements,
    )
    (state_map, state_add, read_map, read_add), local_pull = jax.vjp(
        partial(chunk_terms, keep=keep_block), *prepared_inputs
    )
    before_map, before_add = [None], [None]
    run_map, run_add = state_map[0], state_add[0]
    for number in range(1, block_count):
        before_map.append(run_map)
        before_add.append(run_add)
        run_add = times(run_add, state_map[number]) + state_add[number]
        run_map = times(run_map, state_map[number])
    after_map = [state_map[block_count - 1]]
    for number in range(block_count - 2, -1, -1):
        after_map.append(times(state_map[number], after_map[-1]))
    after_map = after_map[::-1]
    forward_maps = exclusive_maps(run_map, 1)
    backward_maps = exclusive_maps(jnp.swapaxes(run_map, 1, 2), -1)
    start_state = exclusive_chain(forward_maps, run_add, 1)
    states = jnp.concatenate(
        [
            start_state[None],
            jnp.einsum("hij,chjk->chik", start_state, jnp.stack(before_map[1:]), precision=FINE)
            + jnp.stack(before_add[1:]),
        ],
        axis=0,
    )
    read_out = jnp.transpose(
        jnp.einsum("hctj,chij->hcti", read_map, states, precision=FINE).reshape(read_add.shape)
        + read_add,
        (1, 0, 2),
    )
    mixed_f, finish_pull = jax.vjp(
        finish,
        read_out,
        prepared_inputs[0],
        prepared_inputs[4],
        prepared_inputs[5],
        gate_activation,
        attend_elements,
    )
    mixed_low = mixed_f.astype(jnp.bfloat16)
    hidden_in = x_input + swap_sum(back_product(mixed_low, out_turned))
    norm_two, norm_two_pull = jax.vjp(layer_norm, hidden_in, chan_vals[2], chan_vals[3])
    edge_two = from_behind(norm_two[rows_here - 1 :], "seq", 1)
    shift_two = jnp.concatenate([edge_two, norm_two[:-1]], axis=0) * keep_token[:, None] - norm_two
    key_two = (norm_two + shift_two * chan_vals[10]).astype(jnp.bfloat16)
    pre_act = product_matrix(key_two, key_full)
    activated = jnp.square(jax.nn.relu(pre_act)).astype(jnp.bfloat16)
    block_out = hidden_in + swap_sum(back_product(activated, value_turned))
    grad_output = output_gradient.astype(jnp.float32)
    grad_ffo = grad_output.astype(jnp.bfloat16)
    value_sum = halve_sum(weight_grad(grad_ffo, activated), jnp.bfloat16, (1, 0, 3, 2))
    grad_pre = (product_matrix(grad_ffo, value_turned) * 2.0 * jax.nn.relu(pre_act)).astype(
        jnp.bfloat16
    )
    key_sum = halve_sum(weight_grad(key_two, grad_pre), jnp.bfloat16, (0, 1, 3, 2))
    part_key_two = back_product(grad_pre, key_full)
    grad_key_two = swap_sum(part_key_two)
    grad_coeff_two = jnp.sum(grad_key_two * shift_two, axis=0)
    toward_two = grad_key_two * chan_vals[10] * keep_token[:, None]
    back_two = from_behind(toward_two[:1], "seq", -1)
    grad_norm_two = grad_key_two * (1.0 - chan_vals[10]) + jnp.concatenate(
        [toward_two[1:], back_two], axis=0
    )
    grad_hidden, grad_gain_two, grad_bias_two = norm_two_pull(grad_norm_two)
    grad_hidden = grad_hidden + grad_output
    grad_attn = grad_hidden.astype(jnp.bfloat16)
    out_sum = halve_sum(weight_grad(grad_attn, mixed_low), jnp.bfloat16, (1, 0, 3, 2))
    grad_mixed = product_matrix(grad_attn, out_turned)
    grad_read, grad_recv_a, grad_key_a, grad_value_a, grad_gate, grad_head_a = finish_pull(
        grad_mixed
    )
    read_turned = jnp.transpose(grad_read, (1, 0, 2))
    read_blocks = read_turned.reshape(read_map.shape)
    grad_states = jnp.einsum("hcti,hctj->chij", read_blocks, read_map, precision=FINE)
    run_grad = grad_states[block_count - 1]
    after_grad = [jnp.zeros_like(run_grad), run_grad]
    for number in range(block_count - 2, -1, -1):
        run_grad = grad_states[number] + times(run_grad, state_map[number], True)
        after_grad.append(run_grad)
    after_grad = jnp.stack(after_grad[block_count - 1 :: -1])
    grad_end = exclusive_chain(backward_maps, run_grad, -1)
    grad_add = after_grad + jnp.concatenate(
        [
            jnp.einsum("hij,chkj->chik", grad_end, jnp.stack(after_map[1:]), precision=FINE),
            grad_end[None],
        ],
        axis=0,
    )
    grad_map = jnp.einsum("chij,chik->chjk", states, grad_add, precision=FINE)
    grad_read_map = jnp.einsum("hcti,chij->hctj", read_blocks, states, precision=FINE)
    chain_grads = local_pull((grad_map, grad_add, grad_read_map, read_turned))
    cotangents = (
        grad_recv_a + chain_grads[0],
        chain_grads[1],
        chain_grads[2],
        chain_grads[3],
        grad_key_a + chain_grads[4],
        grad_value_a + chain_grads[5],
    )
    (
        grad_recv_raw,
        grad_key_raw,
        grad_value_raw,
        gradient_decay_low_rank,
        gradient_rate_low_rank,
        gradient_value_low_rank,
        grad_first,
        grad_head_b,
    ) = prepare_pull(cotangents)
    recv_round = grad_recv_raw.astype(jnp.bfloat16)
    key_round = grad_key_raw.astype(jnp.bfloat16)
    value_round = grad_value_raw.astype(jnp.bfloat16)
    decay_truncated = gradient_decay_low_rank.astype(jnp.bfloat16)
    rate_truncated = gradient_rate_low_rank.astype(jnp.bfloat16)
    value_low_rank_truncated = gradient_value_low_rank.astype(jnp.bfloat16)
    gate_round = grad_gate.astype(jnp.bfloat16)
    grad_upper = jnp.concatenate(
        [
            weight_grad(decay_truncated, decay_hidden),
            weight_grad(rate_truncated, rate_hidden),
            weight_grad(value_low_rank_truncated, value_hidden),
            weight_grad(gate_round, gate_hid),
        ],
        axis=1,
    )
    mix_sum = halve_sum(
        jnp.concatenate(
            [
                weight_grad(recv_in, recv_round),
                weight_grad(key_in, key_round),
                weight_grad(value_input, value_round),
                halves_side_by_side(grad_upper, half),
            ],
            axis=1,
        ),
        jnp.bfloat16,
        (0, 1, 3, 2),
    )
    part_hidden = jnp.concatenate(
        [
            product_matrix(decay_truncated, up_turned[:, :first_boundary]),
            product_matrix(rate_truncated, up_turned[:, first_boundary:second_boundary]),
            product_matrix(
                value_low_rank_truncated, up_turned[:, second_boundary:third_boundary]
            ),
            product_matrix(gate_round, up_turned[:, third_boundary:]),
        ],
        axis=1,
    )
    part_recv = back_product(recv_round, mix_full[0])
    part_key = back_product(key_round, mix_full[1])
    part_value = back_product(value_round, mix_full[2])
    hidden_sum = swap_sum(part_hidden)
    grad_recv_in = swap_sum(part_recv)
    grad_key_in = swap_sum(part_key)
    grad_value_part = swap_sum(part_value)
    tanh_decay = jnp.tanh(decay_lowrank_output)
    decay_low_round = (hidden_sum[:, :first_boundary] * (1.0 - tanh_decay * tanh_decay)).astype(
        jnp.bfloat16
    )
    rate_low_round = hidden_sum[:, first_boundary:second_boundary].astype(jnp.bfloat16)
    value_low_round = hidden_sum[:, second_boundary:third_boundary].astype(jnp.bfloat16)
    gate_low_round = (hidden_sum[:, third_boundary:] * gate_sig * (1.0 - gate_sig)).astype(
        jnp.bfloat16
    )
    grad_down = jnp.concatenate(
        [
            weight_grad(decay_input, decay_low_round),
            weight_grad(rate_input, rate_low_round),
            weight_grad(value_input, value_low_round),
            weight_grad(gate_input, gate_low_round),
        ],
        axis=1,
    )
    grad_decay_in = back_product(decay_low_round, down_full[:, :first_boundary])
    grad_rate_in = back_product(rate_low_round, down_full[:, first_boundary:second_boundary])
    grad_value_in = grad_value_part + back_product(
        value_low_round, down_full[:, second_boundary:third_boundary]
    )
    grad_gate_in = back_product(gate_low_round, down_full[:, third_boundary:])
    mix_grads = (
        grad_recv_in,
        grad_decay_in,
        grad_key_in,
        grad_value_in,
        grad_rate_in,
        grad_gate_in,
    )
    grad_coeffs = jnp.stack([jnp.sum(gradient * shift_one, axis=0) for gradient in mix_grads])
    direct_one = mix_grads[0] * (1.0 - chan_vals[4])
    toward_one = mix_grads[0] * chan_vals[4]
    for number in range(1, 6):
        direct_one = direct_one + mix_grads[number] * (1.0 - chan_vals[4 + number])
        toward_one = toward_one + mix_grads[number] * chan_vals[4 + number]
    toward_one = toward_one * keep_token[:, None]
    back_one = from_behind(toward_one[:1], "seq", -1)
    grad_norm_one = direct_one + jnp.concatenate([toward_one[1:], back_one], axis=0)
    grad_input, grad_gain_one, grad_bias_one = norm_one_pull(grad_norm_one)
    grad_input = grad_input + grad_hidden
    grad_chan = jnp.concatenate(
        [
            jnp.stack([grad_gain_one, grad_bias_one, grad_gain_two, grad_bias_two]),
            grad_coeffs,
            grad_coeff_two[None],
        ],
        axis=0,
    )
    grad_head = grad_head_a + grad_head_b
    small_sum = halve_sum(
        jnp.concatenate([grad_chan.T, halves_side_by_side(grad_head.T, half)], axis=1),
        jnp.float32,
        (1, 0, 3, 2),
    )
    chan_rows = grad_chan.shape[0]
    down_sum = halve_sum(grad_down, jnp.bfloat16, (1, 0, 3, 2))
    up_sum = halves_stacked(mix_sum[:, 3 * hidden_local :], half)
    return (
        block_out.astype(jnp.bfloat16),
        grad_input,
        grad_first,
        small_sum[:, :chan_rows].T,
        halves_stacked(small_sum[:, chan_rows:], half).T,
        jnp.stack(
            [
                mix_sum[:, number * hidden_local : (number + 1) * hidden_local]
                for number in range(3)
            ]
        ),
        out_sum.T,
        down_sum,
        up_sum.T,
        key_sum,
        value_sum.T,
    )


def solution(mesh):
    in_specs = (
        P("seq", None),
        P("seq", "head"),
        P("seq", None),
        P(),
        P(None, "seq"),
        P(None, ("head", "seq")),
        P(None, "seq", "head"),
        P("head", "seq"),
        P("seq", None),
        P(None, ("head", "seq")),
        P("seq", "head"),
        P("head", "seq"),
    )
    out_specs = (
        P("seq", None),
        P("seq", None),
        P("seq", "head"),
        P(None, "seq"),
        P(None, ("head", "seq")),
        P(None, "seq", "head"),
        P("head", "seq"),
        P("seq", None),
        P(None, ("head", "seq")),
        P("seq", "head"),
        P("head", "seq"),
    )
    return jax.shard_map(shards, mesh=mesh, in_specs=in_specs, out_specs=out_specs, check_vma=False)
```

time: 2440 us -> 717 us (0.29)
  waiting for transfers between devices: 1460 us -> 320 us
  matrix products: 470 us -> 146 us
  blocking collectives: 163 us -> 0 us
  local copies, waits for them, and re-layouts: 175 us -> 71.3 us
  starting transfers between devices: 8.67 us -> 88.8 us
  other arithmetic: 118 us -> 65.2 us
    reduce_scatter x4 -> x0, waiting for transfers between devices: 583 us -> none  [the longest x1 183 us: shards(): lax.psum_scatter(grad_value2, 'seq', scatter_dimension=1, tiled=True)]
    all_gather x8 -> x2, waiting for transfers between devices: 469 us -> 73.6 us  [the longest x1 73.6 us: shards(): first_full = lax.all_gather(first_pack, 'seq', axis=0, tiled=True)]
    unnamed x23 -> x2, waiting for transfers between devices: 357 us -> 0.03 us
    dot_general x451 -> x96, matrix products: 407 us -> 96.8 us  [the longest x77 58.2 us: times(): return jnp.einsum(shape, left, right, precision=FINE)]
    all_gather x4 -> x0, blocking collectives: 160 us -> none  [the longest x1 43.2 us: shards(): lax.all_gather(channel_parameters, 'seq', axis=1, tiled=True)]
    ppermute x4 -> x20, waiting for transfers between devices: 6.61 us -> 154 us  [from_behind(): lax.ppermute(value, axis, [(source, source + steps) for source in range(i...]
    ppermute x0 -> x31, waiting for transfers between devices: none -> 92.1 us  [the longest x24 92.1 us: halve_sum(): lax.ppermute(sent, 'seq', pairs).astype(jnp.float32)]
    dynamic_slice x110 -> x4, local copies, waits for them, and re-layouts: 81.2 us -> 0.12 us  [the longest x2 0.08 us: halve_sum(): kept = lax.dynamic_index_in_dim(held, mine, where, False)]
  transfers between devices with their start and end apart: 23 -> 53, of which waited for: 21 -> 29; matrix products, arithmetic and copies ran while one was open for 5% -> 36% of each run, Pallas kernels for 0% -> 0%
where the time goes in v1:
time: 717 us; the launch traced here: 710 us
  waiting for transfers between devices  320 us (45%)
  matrix products  146 us (20%)
  starting transfers between devices  88.8 us (12%)
  local copies, waits for them, and re-layouts  71.3 us (10%)
  other arithmetic  65.2 us (9%)
  between operations  19.3 us (3%)
    ppermute x20, waiting for transfers between devices, from_behind(): lax.ppermute(value, axis, [(source, source + steps) for source in range(i...  154 us
    ppermute x24, waiting for transfers between devices, halve_sum(): lax.ppermute(sent, 'seq', pairs).astype(jnp.float32)  92.1 us
    all_gather x1, waiting for transfers between devices, shards(): first_full = lax.all_gather(first_pack, 'seq', axis=0, tiled=True)  73.6 us
    ppermute x20, starting transfers between devices, from_behind(): lax.ppermute(value, axis, [(source, source + steps) for source in range(i...  62.7 us
    dot_general x77, matrix products, times(): return jnp.einsum(shape, left, right, precision=FINE)  58.2 us
    ppermute x24, starting transfers between devices, halve_sum(): lax.ppermute(sent, 'seq', pairs).astype(jnp.float32)  24.8 us
    dot_general x9, matrix products, outer(): return jnp.einsum('hcti,hctj->chij', blocks(left), right, precision=FINE)  22.5 us
    dot_general x14, matrix products, product_matrix(): return jnp.dot(operand, weights, preferred_element_type=jnp.float32)  21.8 us
  transfers between devices with their start and end apart: 53, of which 29 were waited for; matrix products, arithmetic and copies ran while one was open for 36% of the time, Pallas kernels for 0%

profile of v1, /device:TPU:0, one launch (start us, length us, event | category | flops | bytes accessed | tf_op | source)
XLA Modules:
  0.0 710.5 jit_solution(10923441471300357372)
XLA Ops:
  17.6 73.6 %all-gather.3.cloned.1.call-done = bf16[1024,1983]{1,0:T(8,128)(2,1)} async-done(((bf16[64,1983]{1,0:T(8,128)(2,1)}), bf16[1024,1983]{1,0:T(8,128)(2,1)}) %all-gather.3.cloned.1.call-update) | async-done | bytes 4061200 | tf_op jit(solution)/shard_map/all_gather | solution.py:268
  92.3 4.4 subtract_reduce_fusion.5
  97.0 3.8 collective-permute-start
  109.2 2.2 fusion.182
  118.3 2.3 multiply_add_fusion.3
  135.8 3.2 fusion.106
  146.0 4.1 collective-permute-start.1
  155.3 2.8 collective-permute-start.3
  172.4 5.4 collective-permute-start.2
  179.3 4.3 collective-permute-start.5
  183.6 6.6 collective-permute-done.2
  190.4 6.5 collective-permute-start.4
  196.9 3.3 collective-permute-done.5
  200.4 7.6 %collective-permute-start.7 = (f32[8,64,64]{2,1,0:T(8,128)S(1)}, f32[8,64,64]{2,1,0:T(8,128)S(1)}, u32[]{:S(2)}, u32[]{:S(2)}) collective-permute-start(f32[8,64,64]{2,1,0:T(8,128)S(1)} %convolution_select_fusion.3), channel_id=1, source_target_pairs={{0,8},{2,10},{4,12},{6,14},{8,16},{10,18},{12,20},{14,22},{16,24},... | collective-permute-start | bytes 393224 | tf_op jit(solution)/shard_map/ppermute | solution.py:22
  208.3 5.7 collective-permute-start.6
  214.0 6.1 collective-permute-done.7
  220.3 8.6 %collective-permute-done.6 = f32[8,64,64]{2,1,0:T(8,128)S(1)} collective-permute-done((f32[8,64,64]{2,1,0:T(8,128)S(1)}, f32[8,64,64]{2,1,0:T(8,128)S(1)}, u32[]{:S(2)}, u32[]{:S(2)}) %collective-permute-start.6) | collective-permute-done | bytes 131104 | tf_op jit(solution)/shard_map/ppermute | solution.py:22
  229.2 2.2 collective-permute-start.8
  232.2 3.1 collective-permute-done.8
  237.4 2.6 fusion.31
  249.2 2.6 fusion.69
  256.9 16.4 %collective-permute-done.19 = f32[8,64,64]{1,2,0:T(8,128)} collective-permute-done((f32[8,64,64]{1,2,0:T(8,128)}, f32[8,64,64]{1,2,0:T(8,128)}, u32[]{:S(2)}, u32[]{:S(2)}) %collective-permute-start.19) | collective-permute-done | bytes 131104 | tf_op jit(solution)/shard_map/ppermute | solution.py:22
  277.9 6.5 collective-permute-start.10
  284.5 11.2 %collective-permute-done.21 = f32[8,64,64]{1,2,0:T(8,128)S(1)} collective-permute-done((f32[8,64,64]{1,2,0:T(8,128)S(1)}, f32[8,64,64]{1,2,0:T(8,128)S(1)}, u32[]{:S(2)}, u32[]{:S(2)}) %collective-permute-start.21) | collective-permute-done | bytes 131104 | tf_op jit(solution)/shard_map/ppermute | solution.py:22
  297.0 3.0 fusion.8
  307.3 2.5 collective-permute-start.43
  315.7 3.0 collective-permute-start.47
  318.8 37.2 %collective-permute-done.13 = f32[1,1024]{1,0:T(1,128)S(1)} collective-permute-done((f32[1,1024]{1,0:T(1,128)S(1)}, f32[1,1024]{1,0:T(1,128)S(1)}, u32[]{:S(2)}, u32[]{:S(2)}) %collective-permute-start.13) | collective-permute-done | bytes 4128 | tf_op jit(solution)/shard_map/ppermute | solution.py:22
  369.9 2.3 fusion.296
  372.1 2.2 fusion.300
  387.8 6.5 collective-permute-done.15
  398.8 5.1 collective-permute-done.16
  419.5 11.0 %collective-permute-done.20 = f32[8,64,64]{2,1,0:T(8,128)S(1)} collective-permute-done((f32[8,64,64]{2,1,0:T(8,128)S(1)}, f32[8,64,64]{2,1,0:T(8,128)S(1)}, u32[]{:S(2)}, u32[]{:S(2)}) %collective-permute-start.20) | collective-permute-done | bytes 131104 | tf_op jit(solution)/shard_map/ppermute | solution.py:22
  433.4 2.9 collective-permute-start.36
  436.3 6.0 collective-permute-done.22
  442.3 2.4 convolution_bitcast_fusion
  445.7 2.5 fusion.40
  448.3 2.5 fusion.34
  452.6 3.6 multiply_reduce_fusion
  458.1 2.2 fusion.218
  460.3 2.6 fusion.216
  464.6 2.5 fusion.27
  469.1 2.4 convolution_multiply_fusion.2
  474.2 2.7 add_convert_fusion.8
  480.1 4.1 fusion.276
  501.8 2.2 fusion.50
  509.0 2.5 fusion.71
  533.1 2.8 collective-permute-start.31
  537.8 2.6 multiply_reduce_fusion.2
  544.0 33.0 %collective-permute-done.26 = f32[1,1024]{1,0:T(1,128)S(1)} collective-permute-done((f32[1,1024]{1,0:T(1,128)S(1)}, f32[1,1024]{1,0:T(1,128)S(1)}, u32[]{:S(2)}, u32[]{:S(2)}) %collective-permute-start.26) | collective-permute-done | bytes 4128 | tf_op jit(solution)/shard_map/ppermute | solution.py:22
  577.0 2.2 fusion.265
  584.6 3.1 collective-permute-done.27
  593.5 3.4 collective-permute-done.29
  602.7 4.9 collective-permute-done.41
  608.4 3.5 collective-permute-done.42
  612.5 3.6 bitcast_add_fusion.1
  616.6 2.7 bitcast_add_fusion
  623.3 19.1 %collective-permute-done.44 = bf16[2,2,64,2048]{3,2,1,0:T(8,128)(2,1)S(1)} collective-permute-done((bf16[2,2,64,2048]{3,2,1,0:T(8,128)(2,1)S(1)}, bf16[2,2,64,2048]{3,2,1,0:T(8,128)(2,1)S(1)}, u32[]{:S(2)}, u32[]{:S(2)}) %collective-permute-start.44) | collective-permute-done | bytes 1048608 | tf_op jit(solution)/shard_map/ppermute | solution.py:73
  643.9 2.5 collective-permute-start.49
  646.3 23.2 %collective-permute-done.45 = bf16[2,64,2048]{2,1,0:T(8,128)(2,1)S(1)} collective-permute-done((bf16[2,64,2048]{2,1,0:T(8,128)(2,1)S(1)}, bf16[2,64,2048]{2,1,0:T(8,128)(2,1)S(1)}, u32[]{:S(2)}, u32[]{:S(2)}) %collective-permute-start.45) | collective-permute-done | bytes 524320 | tf_op jit(solution)/shard_map/ppermute | solution.py:73
  669.8 6.6 collective-permute-done.49
  678.4 8.0 %collective-permute-done.46 = bf16[64,2048]{1,0:T(8,128)(2,1)S(1)} collective-permute-done((bf16[64,2048]{1,0:T(8,128)(2,1)S(1)}, bf16[64,2048]{1,0:T(8,128)(2,1)S(1)}, u32[]{:S(2)}, u32[]{:S(2)}) %collective-permute-start.46) | collective-permute-done | bytes 262176 | tf_op jit(solution)/shard_map/ppermute | solution.py:73
  687.3 8.1 %collective-permute-done.33 = bf16[2,64,1680]{2,1,0:T(8,128)(2,1)S(1)} collective-permute-done((bf16[2,64,1680]{2,1,0:T(8,128)(2,1)S(1)}, bf16[2,64,1680]{2,1,0:T(8,128)(2,1)S(1)}, u32[]{:S(2)}, u32[]{:S(2)}) %collective-permute-start.33) | collective-permute-done | bytes 430112 | tf_op jit(solution)/shard_map/ppermute | solution.py:73
  697.6 4.0 collective-permute-done.34
  (859 shorter events, 248.8 us)
Async XLA Ops:
  7.2 84.0 %all-gather.3.cloned.1.call-start = ((), (), s32[]{:S(2)}) async-start(), calls=%async_computation | async-start | bytes 4456448 | tf_op jit(solution)/shard_map/all_gather | solution.py:268
  12.3 236.9 %all-gather.5.cloned.1.call-start = ((), (), s32[]{:S(2)}) async-start(), calls=%async_computation.1 | async-start | bytes 10027008 | tf_op jit(solution)/shard_map/all_gather | solution.py:272
  14.3 82.5 %copy-start.196 = (s32[128]{0:T(128)}, s32[128]{0:T(128)S(1)}, u32[]{:S(2)}) copy-start(s32[128]{0:T(128)S(1)} %and_select_fusion) | copy-start | bytes 1540
  15.7 89.5 %copy-start.190 = (f32[128]{0:T(128)}, f32[128]{0:T(128)S(1)}, u32[]{:S(2)}) copy-start(f32[128]{0:T(128)S(1)} %broadcast_multiply_fusion.4) | copy-start | bytes 1540
  15.9 89.2 %copy-start.215 = (f32[128]{0:T(128)}, f32[128]{0:T(128)S(1)}, u32[]{:S(2)}) copy-start(f32[128]{0:T(128)S(1)} %fusion.260) | copy-start | bytes 1540
  17.3 79.4 %copy-start.192 = (f32[8]{0:T(128)}, f32[8]{0:T(128)S(1)}, u32[]{:S(2)}) copy-start(f32[8]{0:T(128)S(1)} %fusion.259) | copy-start | bytes 100
  17.5 86.6 %copy-start.212 = (f32[128]{0:T(128)}, f32[128]{0:T(128)S(1)}, u32[]{:S(2)}) copy-start(f32[128]{0:T(128)S(1)} %mul.800) | copy-start | bytes 1540
  97.0 7.0 collective-permute-start
  146.0 25.1 %collective-permute-start.1 = (f32[8,64,64]{2,1,0:T(8,128)}, f32[8,64,64]{2,1,0:T(8,128)}, u32[]{:S(2)}, u32[]{:S(2)}) collective-permute-start(f32[8,64,64]{2,1,0:T(8,128)} %convolution_add_fusion.29), channel_id=1, source_target_pairs={{0,2},{2,4},{4,6},{6,8},{8,10},{10,12},{12,14},{14,16},{16,18},{18... | collective-permute-start | bytes 393224 | tf_op jit(solution)/shard_map/ppermute | solution.py:22
  155.3 22.6 %collective-permute-start.3 = (f32[8,64,64]{2,1,0:T(8,128)}, f32[8,64,64]{2,1,0:T(8,128)}, u32[]{:S(2)}, u32[]{:S(2)}) collective-permute-start(f32[8,64,64]{2,1,0:T(8,128)} %fusion.143), channel_id=1, source_target_pairs={{0,2},{2,4},{4,6},{6,8},{8,10},{10,12},{12,14},{14,16},{16,18},{18... | collective-permute-start | bytes 393224 | tf_op jit(solution)/shard_map/ppermute | solution.py:22
  162.8 88.9 %collective-permute-start.17 = (f32[8,64,64]{1,2,0:T(8,128)}, f32[8,64,64]{1,2,0:T(8,128)}, u32[]{:S(2)}, u32[]{:S(2)}) collective-permute-start(f32[8,64,64]{1,2,0:T(8,128)} %bitcast.109), channel_id=1, source_target_pairs={{2,0},{4,2},{6,4},{8,6},{10,8},{12,10},{14,12},{16,14},{18,16},{20... | collective-permute-start | bytes 393224 | tf_op jit(solution)/shard_map/ppermute | solution.py:22
  172.4 17.7 %collective-permute-start.2 = (f32[8,64,64]{2,1,0:T(8,128)S(1)}, f32[8,64,64]{2,1,0:T(8,128)S(1)}, u32[]{:S(2)}, u32[]{:S(2)}) collective-permute-start(f32[8,64,64]{2,1,0:T(8,128)S(1)} %convolution_add_fusion.28), channel_id=1, source_target_pairs={{0,4},{2,6},{4,8},{6,10},{8,12},{10,14},{12,16},{14,18},{16,20},{1... | collective-permute-start | bytes 393224 | tf_op jit(solution)/shard_map/ppermute | solution.py:22
  179.3 20.9 %collective-permute-start.5 = (f32[8,64,64]{2,1,0:T(8,128)S(1)}, f32[8,64,64]{2,1,0:T(8,128)S(1)}, u32[]{:S(2)}, u32[]{:S(2)}) collective-permute-start(f32[8,64,64]{2,1,0:T(8,128)S(1)} %convolution_select_fusion.4), channel_id=1, source_target_pairs={{0,4},{2,6},{4,8},{6,10},{8,12},{10,14},{12,16},{14,18},{16,20},{1... | collective-permute-start | bytes 393224 | tf_op jit(solution)/shard_map/ppermute | solution.py:22
  190.1 41.3 %copy-start.175 = (f32[8,64]{1,0:T(8,128)S(1)}, f32[8,64]{1,0:T(8,128)}, u32[]{:S(2)}) copy-start(f32[8,64]{1,0:T(8,128)} %mul.857) | copy-start | bytes 6148
  190.4 41.0 %copy-start.19 = (f32[128,512]{0,1:T(8,128)S(1)}, f32[128,512]{0,1:T(8,128)}, u32[]{:S(2)}) copy-start(f32[128,512]{0,1:T(8,128)} %copy-done.18) | copy-start | bytes 786436
  190.4 44.8 %copy-start.86 = (f32[7,8,64,64]{3,2,1,0:T(8,128)S(1)}, f32[7,8,64,64]{3,2,1,0:T(8,128)}, u32[]{:S(2)}) copy-start(f32[7,8,64,64]{3,2,1,0:T(8,128)} %copy-done.85) | copy-start | bytes 2752516
  190.4 44.8 %copy-start.90 = (f32[7,8,64,64]{3,2,1,0:T(8,128)S(1)}, f32[7,8,64,64]{3,2,1,0:T(8,128)}, u32[]{:S(2)}) copy-start(f32[7,8,64,64]{3,2,1,0:T(8,128)} %copy-done.89) | copy-start | bytes 2752516
  190.4 17.6 %collective-permute-start.4 = (f32[8,64,64]{2,1,0:T(8,128)S(1)}, f32[8,64,64]{2,1,0:T(8,128)S(1)}, u32[]{:S(2)}, u32[]{:S(2)}) collective-permute-start(f32[8,64,64]{2,1,0:T(8,128)S(1)} %convolution_add_fusion.27), channel_id=1, source_target_pairs={{0,8},{2,10},{4,12},{6,14},{8,16},{10,18},{12,20},{14,22},{16,24},... | collective-permute-start | bytes 393224 | tf_op jit(solution)/shard_map/ppermute | solution.py:22
  200.4 19.6 %collective-permute-start.7 = (f32[8,64,64]{2,1,0:T(8,128)S(1)}, f32[8,64,64]{2,1,0:T(8,128)S(1)}, u32[]{:S(2)}, u32[]{:S(2)}) collective-permute-start(f32[8,64,64]{2,1,0:T(8,128)S(1)} %convolution_select_fusion.3), channel_id=1, source_target_pairs={{0,8},{2,10},{4,12},{6,14},{8,16},{10,18},{12,20},{14,22},{16,24},... | collective-permute-start | bytes 393224 | tf_op jit(solution)/shard_map/ppermute | solution.py:22
  208.3 20.6 %collective-permute-start.6 = (f32[8,64,64]{2,1,0:T(8,128)S(1)}, f32[8,64,64]{2,1,0:T(8,128)S(1)}, u32[]{:S(2)}, u32[]{:S(2)}) collective-permute-start(f32[8,64,64]{2,1,0:T(8,128)S(1)} %convolution_add_fusion.26), channel_id=1, source_target_pairs={{0,16},{2,18},{4,20},{6,22},{8,24},{10,26},{12,28},{14,30},{1,17},... | collective-permute-start | bytes 393224 | tf_op jit(solution)/shard_map/ppermute | solution.py:22
  229.2 6.0 collective-permute-start.8
  251.8 24.4 %collective-permute-start.9 = (f32[128,1024]{1,0:T(8,128)}, f32[128,1024]{1,0:T(8,128)}, u32[]{:S(2)}, u32[]{:S(2)}) collective-permute-start(f32[128,1024]{1,0:T(8,128)} %fusion.69), channel_id=1, source_target_pairs={{0,1},{1,0},{2,3},{3,2},{4,5},{5,4},{6,7},{7,6},{8,9},{9,8},{10,11... | collective-permute-start | bytes 1572872 | tf_op jit(solution)/shard_map/ppermute | solution.py:26
  253.8 19.5 %collective-permute-start.19 = (f32[8,64,64]{1,2,0:T(8,128)}, f32[8,64,64]{1,2,0:T(8,128)}, u32[]{:S(2)}, u32[]{:S(2)}) collective-permute-start(f32[8,64,64]{1,2,0:T(8,128)} %convolution_select_fusion.5), channel_id=1, source_target_pairs={{4,0},{6,2},{8,4},{10,6},{12,8},{14,10},{16,12},{18,14},{20,16},{2... | collective-permute-start | bytes 393224 | tf_op jit(solution)/shard_map/ppermute | solution.py:22
  274.7 21.0 %collective-permute-start.21 = (f32[8,64,64]{1,2,0:T(8,128)S(1)}, f32[8,64,64]{1,2,0:T(8,128)S(1)}, u32[]{:S(2)}, u32[]{:S(2)}) collective-permute-start(f32[8,64,64]{1,2,0:T(8,128)S(1)} %convolution_select_fusion.1), channel_id=1, source_target_pairs={{8,0},{10,2},{12,4},{14,6},{16,8},{18,10},{20,12},{22,14},{24,16},... | collective-permute-start | bytes 393224 | tf_op jit(solution)/shard_map/ppermute | solution.py:22
  277.9 18.8 %collective-permute-start.10 = (f32[1,1024]{1,0:T(1,128)S(1)}, f32[1,1024]{1,0:T(1,128)S(1)}, u32[]{:S(2)}, u32[]{:S(2)}) collective-permute-start(f32[1,1024]{1,0:T(1,128)S(1)} %slice.491), channel_id=1, source_target_pairs={{0,2},{2,4},{4,6},{6,8},{8,10},{10,12},{12,14},{14,16},{16,18},{18... | collective-permute-start | bytes 12296 | tf_op jit(solution)/shard_map/ppermute | solution.py:22
  303.5 7.6 %collective-permute-start.12 = (f32[128,1024]{1,0:T(8,128)S(1)}, f32[128,1024]{1,0:T(8,128)S(1)}, u32[]{:S(2)}, u32[]{:S(2)}) collective-permute-start(f32[128,1024]{1,0:T(8,128)S(1)} %fusion.4), channel_id=1, source_target_pairs={{0,1},{1,0},{2,3},{3,2},{4,5},{5,4},{6,7},{7,6},{8,9},{9,8},{10,11... | collective-permute-start | bytes 1572872 | tf_op jit(solution)/shard_map/ppermute | solution.py:26
  305.1 51.8 %collective-permute-start.11 = (f32[128,1024]{1,0:T(8,128)S(1)}, f32[128,1024]{1,0:T(8,128)S(1)}, u32[]{:S(2)}, u32[]{:S(2)}) collective-permute-start(f32[128,1024]{1,0:T(8,128)S(1)} %fusion.2), channel_id=1, source_target_pairs={{0,1},{1,0},{2,3},{3,2},{4,5},{5,4},{6,7},{7,6},{8,9},{9,8},{10,11... | collective-permute-start | bytes 1572872 | tf_op jit(solution)/shard_map/ppermute | solution.py:26
  307.3 305.2 %collective-permute-start.43 = (bf16[2,2,2,64,2048]{4,3,1,0,2:T(8,128)(2,1)}, bf16[2,2,2,64,2048]{4,3,1,0,2:T(8,128)(2,1)}, u32[]{:S(2)}, u32[]{:S(2)}) collective-permute-start(bf16[2,2,2,64,2048]{4,3,1,0,2:T(8,128)(2,1)} %fusion.23), channel_id=1, source_target_pairs={{0,2},{2,0},{4,6},{6,4},{8,10},{10,8},{12,14},{14,12},{16,18},{18,... | collective-permute-start | bytes 6291464 | tf_op jit(solution)/shard_map/ppermute | solution.py:73
  311.1 46.7 %copy-start = (f32[2048,1024]{0,1:T(8,128)}, f32[2048,1024]{0,1:T(8,128)S(1)}, u32[]{:S(2)}) copy-start(f32[2048,1024]{0,1:T(8,128)S(1)} %fusion.196) | copy-start | bytes 25165828
  312.4 43.6 %collective-permute-start.13 = (f32[1,1024]{1,0:T(1,128)S(1)}, f32[1,1024]{1,0:T(1,128)S(1)}, u32[]{:S(2)}, u32[]{:S(2)}) collective-permute-start(f32[1,1024]{1,0:T(1,128)S(1)} %slice.497), channel_id=1, source_target_pairs={{2,0},{4,2},{6,4},{8,6},{10,8},{12,10},{14,12},{16,14},{18,16},{20... | collective-permute-start | bytes 12296 | tf_op jit(solution)/shard_map/ppermute | solution.py:22
  314.1 41.9 %copy-start.205 = (f32[1024]{0:T(1024)S(1)}, f32[1024]{0:T(1024)}, u32[]{:S(2)}) copy-start(f32[1024]{0:T(1024)} %get-tuple-element.30) | copy-start | bytes 12292
  315.7 300.8 %collective-permute-start.47 = (bf16[2,2,2,64,2048]{4,3,1,0,2:T(8,128)(2,1)}, bf16[2,2,2,64,2048]{4,3,1,0,2:T(8,128)(2,1)}, u32[]{:S(2)}, u32[]{:S(2)}) collective-permute-start(bf16[2,2,2,64,2048]{4,3,1,0,2:T(8,128)(2,1)} %fusion.24), channel_id=1, source_target_pairs={{0,4},{2,6},{4,0},{6,2},{8,12},{10,14},{12,8},{14,10},{16,20},{18,... | collective-permute-start | bytes 6291464 | tf_op jit(solution)/shard_map/ppermute | solution.py:73
  383.4 10.9 %collective-permute-start.15 = (f32[8,64,64]{2,1,0:T(8,128)S(1)}, f32[8,64,64]{2,1,0:T(8,128)S(1)}, u32[]{:S(2)}, u32[]{:S(2)}) collective-permute-start(f32[8,64,64]{2,1,0:T(8,128)S(1)} %convolution_add_fusion.16), channel_id=1, source_target_pairs={{2,0},{4,2},{6,4},{8,6},{10,8},{12,10},{14,12},{16,14},{18,16},{20... | collective-permute-start | bytes 393224 | tf_op jit(solution)/shard_map/ppermute | solution.py:22
  395.6 8.3 %collective-permute-start.16 = (f32[8,64,64]{2,1,0:T(8,128)S(1)}, f32[8,64,64]{2,1,0:T(8,128)S(1)}, u32[]{:S(2)}, u32[]{:S(2)}) collective-permute-start(f32[8,64,64]{2,1,0:T(8,128)S(1)} %convolution_add_fusion.15), channel_id=1, source_target_pairs={{4,0},{6,2},{8,4},{10,6},{12,8},{14,10},{16,12},{18,14},{20,16},{2... | collective-permute-start | bytes 393224 | tf_op jit(solution)/shard_map/ppermute | solution.py:22
  405.9 9.1 %collective-permute-start.18 = (f32[8,64,64]{2,1,0:T(8,128)}, f32[8,64,64]{2,1,0:T(8,128)}, u32[]{:S(2)}, u32[]{:S(2)}) collective-permute-start(f32[8,64,64]{2,1,0:T(8,128)} %convolution_add_fusion.14), channel_id=1, source_target_pairs={{8,0},{10,2},{12,4},{14,6},{16,8},{18,10},{20,12},{22,14},{24,16},... | collective-permute-start | bytes 393224 | tf_op jit(solution)/shard_map/ppermute | solution.py:22
  412.2 20.2 %collective-permute-start.35 = (bf16[2,2,2,64,512]{4,3,1,0,2:T(8,128)(2,1)}, bf16[2,2,2,64,512]{4,3,1,0,2:T(8,128)(2,1)S(1)}, u32[]{:S(2)}, u32[]{:S(2)}) collective-permute-start(bf16[2,2,2,64,512]{4,3,1,0,2:T(8,128)(2,1)} %fusion.96), channel_id=1, source_target_pairs={{0,4},{2,6},{4,0},{6,2},{8,12},{10,14},{12,8},{14,10},{16,20},{18,... | collective-permute-start | bytes 1572872 | tf_op jit(solution)/shard_map/ppermute | solution.py:73
  416.5 14.1 %collective-permute-start.20 = (f32[8,64,64]{2,1,0:T(8,128)S(1)}, f32[8,64,64]{2,1,0:T(8,128)S(1)}, u32[]{:S(2)}, u32[]{:S(2)}) collective-permute-start(f32[8,64,64]{2,1,0:T(8,128)S(1)} %convolution_add_fusion.13), channel_id=1, source_target_pairs={{16,0},{18,2},{20,4},{22,6},{24,8},{26,10},{28,12},{30,14},{17,1},... | collective-permute-start | bytes 393224 | tf_op jit(solution)/shard_map/ppermute | solution.py:22
  430.9 11.4 %collective-permute-start.22 = (f32[8,64,64]{2,1,0:T(8,128)S(1)}, f32[8,64,64]{2,1,0:T(8,128)S(1)}, u32[]{:S(2)}, u32[]{:S(2)}) collective-permute-start(f32[8,64,64]{2,1,0:T(8,128)S(1)} %convolution_add_fusion.12), channel_id=1, source_target_pairs={{2,0},{4,2},{6,4},{8,6},{10,8},{12,10},{14,12},{16,14},{18,16},{20... | collective-permute-start | bytes 393224 | tf_op jit(solution)/shard_map/ppermute | solution.py:22
  433.4 89.6 %collective-permute-start.36 = (bf16[2,2,64,512]{3,2,1,0:T(8,128)(2,1)}, bf16[2,2,64,512]{3,2,1,0:T(8,128)(2,1)}, u32[]{:S(2)}, u32[]{:S(2)}) collective-permute-start(bf16[2,2,64,512]{3,2,1,0:T(8,128)(2,1)} %fusion.123), channel_id=1, source_target_pairs={{0,2},{2,0},{4,6},{6,4},{8,10},{10,8},{12,14},{14,12},{16,18},{18,... | collective-permute-start | bytes 786440 | tf_op jit(solution)/shard_map/ppermute | solution.py:73
  508.5 16.4 %collective-permute-start.23 = (f32[128,288]{0,1:T(8,128)}, f32[128,288]{0,1:T(8,128)}, u32[]{:S(2)}, u32[]{:S(2)}) collective-permute-start(f32[128,288]{0,1:T(8,128)} %pad_maximum_fusion.8), channel_id=1, source_target_pairs={{0,1},{1,0},{2,3},{3,2},{4,5},{5,4},{6,7},{7,6},{8,9},{9,8},{10,11... | collective-permute-start | bytes 442376 | tf_op jit(solution)/shard_map/ppermute | solution.py:26
  511.5 21.6 %collective-permute-start.25 = (f32[128,1024]{1,0:T(8,128)}, f32[128,1024]{1,0:T(8,128)}, u32[]{:S(2)}, u32[]{:S(2)}) collective-permute-start(f32[128,1024]{1,0:T(8,128)} %fusion.71), channel_id=1, source_target_pairs={{0,1},{1,0},{2,3},{3,2},{4,5},{5,4},{6,7},{7,6},{8,9},{9,8},{10,11... | collective-permute-start | bytes 1572872 | tf_op jit(solution)/shard_map/ppermute | solution.py:26
  523.0 14.5 %collective-permute-start.24 = (f32[128,1024]{1,0:T(8,128)S(1)}, f32[128,1024]{1,0:T(8,128)}, u32[]{:S(2)}, u32[]{:S(2)}) collective-permute-start(f32[128,1024]{1,0:T(8,128)S(1)} %fusion.75), channel_id=1, source_target_pairs={{0,1},{1,0},{2,3},{3,2},{4,5},{5,4},{6,7},{7,6},{8,9},{9,8},{10,11... | collective-permute-start | bytes 1572872 | tf_op jit(solution)/shard_map/ppermute | solution.py:26
  524.9 7.1 %collective-permute-start.37 = (bf16[2,64,512]{2,1,0:T(8,128)(2,1)}, bf16[2,64,512]{2,1,0:T(8,128)(2,1)}, u32[]{:S(2)}, u32[]{:S(2)}) collective-permute-start(bf16[2,64,512]{2,1,0:T(8,128)(2,1)} %fusion.200), channel_id=1, source_target_pairs={{0,16},{2,18},{4,20},{6,22},{8,24},{10,26},{12,28},{14,30},{16,0},... | collective-permute-start | bytes 393224 | tf_op jit(solution)/shard_map/ppermute | solution.py:73
  532.0 5.6 collective-permute-start.14
  533.1 86.4 %collective-permute-start.31 = (bf16[2,2,2,64,1680]{4,3,2,1,0:T(8,128)(2,1)}, bf16[2,2,2,64,1680]{4,3,2,1,0:T(8,128)(2,1)}, u32[]{:S(2)}, u32[]{:S(2)}) collective-permute-start(bf16[2,2,2,64,1680]{4,3,2,1,0:T(8,128)(2,1)} %fusion.33), channel_id=1, source_target_pairs={{0,2},{2,0},{4,6},{6,4},{8,10},{10,8},{12,14},{14,12},{16,18},{18,... | collective-permute-start | bytes 5160968 | tf_op jit(solution)/shard_map/ppermute | solution.py:73
  537.5 46.0 %collective-permute-start.39 = (bf16[2,2,2,64,288]{4,3,2,1,0:T(8,128)(2,1)}, bf16[2,2,2,64,288]{4,3,2,1,0:T(8,128)(2,1)}, u32[]{:S(2)}, u32[]{:S(2)}) collective-permute-start(bf16[2,2,2,64,288]{4,3,2,1,0:T(8,128)(2,1)} %fusion.112), channel_id=1, source_target_pairs={{0,4},{2,6},{4,0},{6,2},{8,12},{10,14},{12,8},{14,10},{16,20},{18,... | collective-permute-start | bytes 884744 | tf_op jit(solution)/shard_map/ppermute | solution.py:73
  537.6 4.3 collective-permute-start.38
  541.9 35.0 %collective-permute-start.26 = (f32[1,1024]{1,0:T(1,128)S(1)}, f32[1,1024]{1,0:T(1,128)S(1)}, u32[]{:S(2)}, u32[]{:S(2)}) collective-permute-start(f32[1,1024]{1,0:T(1,128)S(1)} %slice.511), channel_id=1, source_target_pairs={{2,0},{4,2},{6,4},{8,6},{10,8},{12,10},{14,12},{16,14},{18,16},{20... | collective-permute-start | bytes 12296 | tf_op jit(solution)/shard_map/ppermute | solution.py:22
  583.5 4.3 collective-permute-start.27
  587.9 4.2 collective-permute-start.28
  588.0 13.3 %collective-permute-start.40 = (bf16[2,2,64,288]{3,2,1,0:T(8,128)(2,1)S(1)}, bf16[2,2,64,288]{3,2,1,0:T(8,128)(2,1)S(1)}, u32[]{:S(2)}, u32[]{:S(2)}) collective-permute-start(bf16[2,2,64,288]{3,2,1,0:T(8,128)(2,1)S(1)} %fusion.197), channel_id=1, source_target_pairs={{0,2},{2,0},{4,6},{6,4},{8,10},{10,8},{12,14},{14,12},{16,18},{18,... | collective-permute-start | bytes 442376 | tf_op jit(solution)/shard_map/ppermute | solution.py:73
  592.2 4.7 collective-permute-start.29
  596.9 3.7 collective-permute-start.30
  601.3 6.3 collective-permute-start.41
  607.7 4.2 collective-permute-start.42
  616.3 26.2 %collective-permute-start.44 = (bf16[2,2,64,2048]{3,2,1,0:T(8,128)(2,1)S(1)}, bf16[2,2,64,2048]{3,2,1,0:T(8,128)(2,1)S(1)}, u32[]{:S(2)}, u32[]{:S(2)}) collective-permute-start(bf16[2,2,64,2048]{3,2,1,0:T(8,128)(2,1)S(1)} %fusion.65), channel_id=1, source_target_pairs={{0,4},{2,6},{4,0},{6,2},{8,12},{10,14},{12,8},{14,10},{16,20},{18,... | collective-permute-start | bytes 3145736 | tf_op jit(solution)/shard_map/ppermute | solution.py:73
  619.4 24.1 %collective-permute-start.48 = (bf16[2,2,64,2048]{3,2,1,0:T(8,128)(2,1)S(1)}, bf16[2,2,64,2048]{3,2,1,0:T(8,128)(2,1)S(1)}, u32[]{:S(2)}, u32[]{:S(2)}) collective-permute-start(bf16[2,2,64,2048]{3,2,1,0:T(8,128)(2,1)S(1)} %fusion.66), channel_id=1, source_target_pairs={{0,2},{2,0},{4,6},{6,4},{8,10},{10,8},{12,14},{14,12},{16,18},{18,... | collective-permute-start | bytes 3145736 | tf_op jit(solution)/shard_map/ppermute | solution.py:73
  622.0 54.7 %collective-permute-start.32 = (bf16[2,2,64,1680]{3,2,1,0:T(8,128)(2,1)S(1)}, bf16[2,2,64,1680]{3,2,1,0:T(8,128)(2,1)S(1)}, u32[]{:S(2)}, u32[]{:S(2)}) collective-permute-start(bf16[2,2,64,1680]{3,2,1,0:T(8,128)(2,1)S(1)} %fusion.83), channel_id=1, source_target_pairs={{0,4},{2,6},{4,0},{6,2},{8,12},{10,14},{12,8},{14,10},{16,20},{18,... | collective-permute-start | bytes 2580488 | tf_op jit(solution)/shard_map/ppermute | solution.py:73
  642.9 26.7 %collective-permute-start.45 = (bf16[2,64,2048]{2,1,0:T(8,128)(2,1)S(1)}, bf16[2,64,2048]{2,1,0:T(8,128)(2,1)S(1)}, u32[]{:S(2)}, u32[]{:S(2)}) collective-permute-start(bf16[2,64,2048]{2,1,0:T(8,128)(2,1)S(1)} %fusion.94), channel_id=1, source_target_pairs={{0,16},{2,18},{4,20},{6,22},{8,24},{10,26},{12,28},{14,30},{16,0},... | collective-permute-start | bytes 1572872 | tf_op jit(solution)/shard_map/ppermute | solution.py:73
  643.9 32.5 %collective-permute-start.49 = (bf16[2,64,2048]{2,1,0:T(8,128)(2,1)S(1)}, bf16[2,64,2048]{2,1,0:T(8,128)(2,1)S(1)}, u32[]{:S(2)}, u32[]{:S(2)}) collective-permute-start(bf16[2,64,2048]{2,1,0:T(8,128)(2,1)S(1)} %fusion.95), channel_id=1, source_target_pairs={{0,16},{2,18},{4,20},{6,22},{8,24},{10,26},{12,28},{14,30},{16,0},... | collective-permute-start | bytes 1572872 | tf_op jit(solution)/shard_map/ppermute | solution.py:73
  669.7 16.7 %collective-permute-start.46 = (bf16[64,2048]{1,0:T(8,128)(2,1)S(1)}, bf16[64,2048]{1,0:T(8,128)(2,1)S(1)}, u32[]{:S(2)}, u32[]{:S(2)}) collective-permute-start(bf16[64,2048]{1,0:T(8,128)(2,1)S(1)} %fusion.124), channel_id=1, source_target_pairs={{0,8},{2,10},{4,12},{6,14},{8,0},{10,2},{12,4},{14,6},{16,24},{18,... | collective-permute-start | bytes 786440 | tf_op jit(solution)/shard_map/ppermute | solution.py:73
  676.6 20.2 %collective-permute-start.50 = (bf16[64,2048]{1,0:T(8,128)(2,1)S(1)}, bf16[64,2048]{1,0:T(8,128)(2,1)S(1)}, u32[]{:S(2)}, u32[]{:S(2)}) collective-permute-start(bf16[64,2048]{1,0:T(8,128)(2,1)S(1)} %fusion.125), channel_id=1, source_target_pairs={{0,8},{2,10},{4,12},{6,14},{8,0},{10,2},{12,4},{14,6},{16,24},{18,... | collective-permute-start | bytes 786440 | tf_op jit(solution)/shard_map/ppermute | solution.py:73
  676.9 18.5 %collective-permute-start.33 = (bf16[2,64,1680]{2,1,0:T(8,128)(2,1)S(1)}, bf16[2,64,1680]{2,1,0:T(8,128)(2,1)S(1)}, u32[]{:S(2)}, u32[]{:S(2)}) collective-permute-start(bf16[2,64,1680]{2,1,0:T(8,128)(2,1)S(1)} %fusion.111), channel_id=1, source_target_pairs={{0,16},{2,18},{4,20},{6,22},{8,24},{10,26},{12,28},{14,30},{16,0},... | collective-permute-start | bytes 1290248 | tf_op jit(solution)/shard_map/ppermute | solution.py:73
  695.5 6.1 collective-permute-start.34
  (221 other events, 1500.3 us)
Sparse Core Ops, SparseCore 0:
  12.4 78.7 all-gather.2
  94.0 137.6 all-gather.4

commit v2 on v1

--- a/solution.py
+++ b/solution.py
@@ -35,43 +35,58 @@
     return [1 << power for power in range((count - 1).bit_length())]
 
 
-def exclusive_maps(own_map, direction):
+def exclusive_chain(own_map, own_add, direction):
     count = lax.axis_size("seq")
     place = lax.axis_index("seq")
     behind = place if direction > 0 else count - 1 - place
-    maps = []
-    total = own_map
+    width = own_map.shape[1]
+    total = jnp.concatenate([jnp.swapaxes(own_map, 1, 2), jnp.swapaxes(own_add, 1, 2)], axis=2)
+    from_map = (jnp.arange(2 * width) < width)[None, None]
     for step in chain_steps(count):
-        maps.append(total)
-        if 2 * step < count:
-            arrived = from_behind(total, "seq", direction * step)
-            total = jnp.where(behind >= step, times(arrived, total), total)
-    return maps
-
-
-def exclusive_chain(maps, own_add, direction):
-    total = own_add
-    for step, step_map in zip(chain_steps(lax.axis_size("seq")), maps):
         arrived = from_behind(total, "seq", direction * step)
-        total = total + times(arrived, step_map)
-    return from_behind(total, "seq", direction)
-
-
-def halve_sum(rows, sent_type, order):
+        moved = times(total[:, :, :width], arrived)
+        total = jnp.where(from_map & (behind >= step), 0.0, total) + jnp.where(
+            from_map & (behind < step), 0.0, moved
+        )
+    return jnp.swapaxes(from_behind(total[:, :, width:], "seq", direction), 1, 2)
+
+
+def halve_order(first):
+    bits = (lax.axis_size("seq") - 1).bit_length()
+    order = list(range(bits))
+    return order[first::-1] + order[first + 1 :]
+
+
+def halve_start(rows):
     count = lax.axis_size("seq")
-    place = lax.axis_index("seq")
     bits = (count - 1).bit_length()
-    left = list(range(bits - 1, -1, -1))
-    held = rows.reshape((2,) * bits + (rows.shape[0] // count, rows.shape[1]))
-    for bit in [number for number in order if number < bits] + list(range(len(order), bits)):
-        where = left.index(bit)
-        left.remove(bit)
-        mine = (place >> bit) & 1
-        kept = lax.dynamic_index_in_dim(held, mine, where, False)
-        sent = lax.dynamic_index_in_dim(held, 1 - mine, where, False).astype(sent_type)
-        pairs = [(number, number ^ (1 << bit)) for number in range(count)]
-        held = kept.astype(jnp.float32) + lax.ppermute(sent, "seq", pairs).astype(jnp.float32)
+    return rows.reshape((2,) * bits + (rows.shape[0] // count, rows.shape[1]))
+
+
+def halve_step(held, order, number, sent_type, after=None):
+    count = lax.axis_size("seq")
+    bit = order[number]
+    where = sorted(order[number:], reverse=True).index(bit)
+    mine = (lax.axis_index("seq") >> bit) & 1
+    kept = lax.dynamic_index_in_dim(held, mine, where, False)
+    sent = lax.dynamic_index_in_dim(held, 1 - mine, where, False)
+    if after is not None:
+        sent = sent + after
+    pairs = [(place, place ^ (1 << bit)) for place in range(count)]
+    arrived = lax.ppermute(sent.astype(sent_type), "seq", pairs)
+    return kept.astype(jnp.float32) + arrived.astype(jnp.float32)
+
+
+def halve_sum(rows, sent_type, first, after=None):
+    order = halve_order(first)
+    held = halve_start(rows)
+    for number in range(len(order)):
+        held = halve_step(held, order, number, sent_type, after if number == 0 else None)
     return held
+
+
+def order_mark(value):
+    return value[(0,) * value.ndim].astype(jnp.float32) * 0.0
 
 
 def halves_side_by_side(rows, width):
@@ -356,9 +371,7 @@
     for number in range(block_count - 2, -1, -1):
         after_map.append(times(state_map[number], after_map[-1]))
     after_map = after_map[::-1]
-    forward_maps = exclusive_maps(run_map, 1)
-    backward_maps = exclusive_maps(jnp.swapaxes(run_map, 1, 2), -1)
-    start_state = exclusive_chain(forward_maps, run_add, 1)
+    start_state = exclusive_chain(run_map, run_add, 1)
     states = jnp.concatenate(
         [
             start_state[None],
@@ -392,23 +405,27 @@
     block_out = hidden_in + swap_sum(back_product(activated, value_turned))
     grad_output = output_gradient.astype(jnp.float32)
     grad_ffo = grad_output.astype(jnp.bfloat16)
-    value_sum = halve_sum(weight_grad(grad_ffo, activated), jnp.bfloat16, (1, 0, 3, 2))
+    value_held = halve_start(weight_grad(grad_ffo, activated))
     grad_pre = (product_matrix(grad_ffo, value_turned) * 2.0 * jax.nn.relu(pre_act)).astype(
         jnp.bfloat16
     )
-    key_sum = halve_sum(weight_grad(key_two, grad_pre), jnp.bfloat16, (0, 1, 3, 2))
+    key_held = halve_start(weight_grad(key_two, grad_pre))
     part_key_two = back_product(grad_pre, key_full)
     grad_key_two = swap_sum(part_key_two)
     grad_coeff_two = jnp.sum(grad_key_two * shift_two, axis=0)
     toward_two = grad_key_two * chan_vals[10] * keep_token[:, None]
     back_two = from_behind(toward_two[:1], "seq", -1)
+    key_order, value_order = halve_order(0), halve_order(1)
+    edge_mark = order_mark(back_two)
+    key_held = halve_step(key_held, key_order, 0, jnp.bfloat16, edge_mark)
+    value_held = halve_step(value_held, value_order, 0, jnp.bfloat16, edge_mark)
     grad_norm_two = grad_key_two * (1.0 - chan_vals[10]) + jnp.concatenate(
         [toward_two[1:], back_two], axis=0
     )
     grad_hidden, grad_gain_two, grad_bias_two = norm_two_pull(grad_norm_two)
     grad_hidden = grad_hidden + grad_output
     grad_attn = grad_hidden.astype(jnp.bfloat16)
-    out_sum = halve_sum(weight_grad(grad_attn, mixed_low), jnp.bfloat16, (1, 0, 3, 2))
+    grad_out_turned = weight_grad(grad_attn, mixed_low)
     grad_mixed = product_matrix(grad_attn, out_turned)
     grad_read, grad_recv_a, grad_key_a, grad_value_a, grad_gate, grad_head_a = finish_pull(
         grad_mixed
@@ -422,7 +439,7 @@
         run_grad = grad_states[number] + times(run_grad, state_map[number], True)
         after_grad.append(run_grad)
     after_grad = jnp.stack(after_grad[block_count - 1 :: -1])
-    grad_end = exclusive_chain(backward_maps, run_grad, -1)
+    grad_end = exclusive_chain(jnp.swapaxes(run_map, 1, 2), run_grad, -1)
     grad_add = after_grad + jnp.concatenate(
         [
             jnp.einsum("hij,chkj->chik", grad_end, jnp.stack(after_map[1:]), precision=FINE),
@@ -472,14 +489,21 @@
             [
                 weight_grad(recv_in, recv_round),
                 weight_grad(key_in, key_round),
-                weight_grad(value_input, value_round),
                 halves_side_by_side(grad_upper, half),
             ],
             axis=1,
         ),
         jnp.bfloat16,
-        (0, 1, 3, 2),
-    )
+        0,
+    )
+    rest_sum = halve_sum(
+        jnp.concatenate([weight_grad(value_input, value_round), grad_out_turned], axis=1),
+        jnp.bfloat16,
+        1,
+    )
+    for number in range(1, len(key_order)):
+        key_held = halve_step(key_held, key_order, number, jnp.bfloat16)
+        value_held = halve_step(value_held, value_order, number, jnp.bfloat16)
     part_hidden = jnp.concatenate(
         [
             product_matrix(decay_truncated, up_turned[:, :first_boundary]),
@@ -551,30 +575,30 @@
     )
     grad_head = grad_head_a + grad_head_b
     small_sum = halve_sum(
-        jnp.concatenate([grad_chan.T, halves_side_by_side(grad_head.T, half)], axis=1),
+        jnp.concatenate([grad_down, grad_chan.T, halves_side_by_side(grad_head.T, half)], axis=1),
         jnp.float32,
-        (1, 0, 3, 2),
-    )
-    chan_rows = grad_chan.shape[0]
-    down_sum = halve_sum(grad_down, jnp.bfloat16, (1, 0, 3, 2))
-    up_sum = halves_stacked(mix_sum[:, 3 * hidden_local :], half)
+        1,
+    )
+    place_head = low_columns + grad_chan.shape[0]
+    up_sum = halves_stacked(mix_sum[:, 2 * hidden_local :], half)
     return (
         block_out.astype(jnp.bfloat16),
         grad_input,
         grad_first,
-        small_sum[:, :chan_rows].T,
-        halves_stacked(small_sum[:, chan_rows:], half).T,
+        small_sum[:, low_columns:place_head].T,
+        halves_stacked(small_sum[:, place_head:], half).T,
         jnp.stack(
             [
-                mix_sum[:, number * hidden_local : (number + 1) * hidden_local]
-                for number in range(3)
+                mix_sum[:, :hidden_local],
+                mix_sum[:, hidden_local : 2 * hidden_local],
+                rest_sum[:, :hidden_local],
             ]
         ),
-        out_sum.T,
-        down_sum,
+        rest_sum[:, hidden_local:].T,
+        small_sum[:, :low_columns],
         up_sum.T,
-        key_sum,
-        value_sum.T,
+        key_held,
+        value_held.T,
     )
 
 

time: 717 us -> 711 us (level)
  waiting for transfers between devices: 320 us -> 228 us
  local copies, waits for them, and re-layouts: 71.3 us -> 112 us
  other arithmetic: 65.2 us -> 85.7 us
  starting transfers between devices: 88.8 us -> 102 us
  matrix products: 146 us -> 157 us
    ppermute x20 -> x14, waiting for transfers between devices: 154 us -> 80.8 us  [from_behind(): lax.ppermute(value, axis, [(source, source + steps) for source in range(i...]
    ppermute x24 -> x20, waiting for transfers between devices: 92.1 us -> 78.4 us  [halve_step(): arrived = lax.ppermute(sent.astype(sent_type), 'seq', pairs)]
    dynamic_slice x4 -> x7, local copies, waits for them, and re-layouts: 0.12 us -> 11.2 us  [the longest x4 8.7 us: halve_step(): sent = lax.dynamic_index_in_dim(held, 1 - mine, where, False)]
    concatenate x2 -> x4, local copies, waits for them, and re-layouts: 0.58 us -> 10.3 us  [the longest x1 5.56 us: shards(): jnp.concatenate([weight_grad(value_input, value_round), grad_out_turned],...]
    and x0 -> x16, other arithmetic: none -> 8.72 us  [the longest x8 4.44 us: exclusive_chain(): from_map & (behind < step)]
    ppermute x24 -> x20, starting transfers between devices: 24.8 us -> 33 us  [halve_step(): arrived = lax.ppermute(sent.astype(sent_type), 'seq', pairs)]
    unnamed x481 -> x523, local copies, waits for them, and re-layouts: 12.8 us -> 19 us
    add x22 -> x21, other arithmetic: 14.4 us -> 19.6 us  [the longest x19 18.2 us: halve_step(): return kept.astype(jnp.float32) + arrived.astype(jnp.float32)]
  transfers between devices with their start and end apart: 53 -> 43, of which waited for: 29 -> 19; matrix products, arithmetic and copies ran while one was open for 36% -> 42% of each run, Pallas kernels for 0% -> 0%
where the time goes in v2:
time: 711 us; the launch traced here: 704 us
  waiting for transfers between devices  228 us (32%)
  matrix products  157 us (22%)
  local copies, waits for them, and re-layouts  112 us (16%)
  starting transfers between devices  102 us (14%)
  other arithmetic  85.7 us (12%)
  between operations  19.5 us (3%)
    ppermute x14, waiting for transfers between devices, from_behind(): lax.ppermute(value, axis, [(source, source + steps) for source in range(i...  80.8 us
    ppermute x20, waiting for transfers between devices, halve_step(): arrived = lax.ppermute(sent.astype(sent_type), 'seq', pairs)  78.4 us
    all_gather x1, waiting for transfers between devices, shards(): first_full = lax.all_gather(first_pack, 'seq', axis=0, tiled=True)  68.7 us
    ppermute x14, starting transfers between devices, from_behind(): lax.ppermute(value, axis, [(source, source + steps) for source in range(i...  67.4 us
    dot_general x71, matrix products, times(): return jnp.einsum(shape, left, right, precision=FINE)  59.9 us
    ppermute x20, starting transfers between devices, halve_step(): arrived = lax.ppermute(sent.astype(sent_type), 'seq', pairs)  33 us
    dot_general x9, matrix products, outer(): return jnp.einsum('hcti,hctj->chij', blocks(left), right, precision=FINE)  23 us
    dot_general x14, matrix products, product_matrix(): return jnp.dot(operand, weights, preferred_element_type=jnp.float32)  20.9 us
  transfers between devices with their start and end apart: 43, of which 19 were waited for; matrix products, arithmetic and copies ran while one was open for 42% of the time, Pallas kernels for 0%

profile of v2, /device:TPU:0, one launch (start us, length us, event | category | flops | bytes accessed | tf_op | source)
XLA Modules:
  0.0 703.8 jit_solution(4466967567107637840)
XLA Ops:
  22.5 68.7 %all-gather.3.cloned.1.call-done = bf16[1024,1983]{1,0:T(8,128)(2,1)} async-done(((bf16[64,1983]{1,0:T(8,128)(2,1)}), bf16[1024,1983]{1,0:T(8,128)(2,1)}) %all-gather.3.cloned.1.call-update) | async-done | bytes 4061200 | tf_op jit(solution)/shard_map/all_gather | solution.py:283
  92.3 4.4 subtract_reduce_fusion.5
  97.0 3.6 collective-permute-start
  111.0 2.3 multiply_add_fusion.3
  129.3 2.8 add_multiply_fusion
  143.8 3.1 fusion.112
  153.3 4.1 collective-permute-start.1
  163.2 3.7 collective-permute-done.1
  168.4 5.4 collective-permute-start.2
  176.9 6.4 collective-permute-done.2
  183.6 7.9 %collective-permute-start.3 = (f32[8,64,128]{2,1,0:T(8,128)S(1)}, f32[8,64,128]{2,1,0:T(8,128)S(1)}, u32[]{:S(2)}, u32[]{:S(2)}) collective-permute-start(f32[8,64,128]{2,1,0:T(8,128)S(1)} %select_add_fusion.3), channel_id=1, source_target_pairs={{0,8},{2,10},{4,12},{6,14},{8,16},{10,18},{12,20},{14,22},{16,24},... | collective-permute-start | bytes 786440 | tf_op jit(solution)/shard_map/ppermute | solution.py:22
  194.2 3.5 collective-permute-done.3
  198.7 28.9 %collective-permute-start.4 = (f32[8,64,128]{2,1,0:T(8,128)}, f32[8,64,128]{2,1,0:T(8,128)}, u32[]{:S(2)}, u32[]{:S(2)}) collective-permute-start(f32[8,64,128]{2,1,0:T(8,128)} %select_add_fusion.2), channel_id=1, source_target_pairs={{0,16},{2,18},{4,20},{6,22},{8,24},{10,26},{12,28},{14,30},{1,17},... | collective-permute-start | bytes 786440 | tf_op jit(solution)/shard_map/ppermute | solution.py:22
  231.6 2.6 convolution_add_fusion.20
  236.7 2.7 collective-permute-start.5
  240.2 3.1 collective-permute-done.5
  243.3 3.3 bitcast_add_fusion.6
  247.8 2.4 fusion.29
  264.3 5.0 collective-permute-start.7
  275.3 3.0 fusion.10
  278.3 3.1 fusion.22
  287.1 3.8 constant_dynamic-slice_fusion.2
  295.6 3.8 constant_dynamic-slice_fusion
  302.4 2.9 fusion.283
  314.6 2.2 fusion.313
  324.0 2.6 fusion.107
  341.4 3.1 fusion.47
  349.7 3.3 collective-permute-start.33
  353.3 4.4 collective-permute-done.13
  360.9 7.3 %collective-permute-done.14 = f32[8,64,128]{2,1,0:T(8,128)S(1)} collective-permute-done((f32[8,64,128]{2,1,0:T(8,128)S(1)}, f32[8,64,128]{2,1,0:T(8,128)S(1)}, u32[]{:S(2)}, u32[]{:S(2)}) %collective-permute-start.14) | collective-permute-done | bytes 262176 | tf_op jit(solution)/shard_map/ppermute | solution.py:22
  372.4 2.3 collective-permute-start.37
  375.7 8.3 %collective-permute-done.15 = f32[8,64,128]{2,1,0:T(8,128)S(1)} collective-permute-done((f32[8,64,128]{2,1,0:T(8,128)S(1)}, f32[8,64,128]{2,1,0:T(8,128)S(1)}, u32[]{:S(2)}, u32[]{:S(2)}) %collective-permute-start.15) | collective-permute-done | bytes 262176 | tf_op jit(solution)/shard_map/ppermute | solution.py:22
  386.7 17.9 %collective-permute-done.16 = f32[8,64,64]{2,1,0:T(8,128)S(1)} collective-permute-done((f32[8,64,64]{2,1,0:T(8,128)S(1)}, f32[8,64,64]{2,1,0:T(8,128)S(1)}, u32[]{:S(2)}, u32[]{:S(2)}) %collective-permute-start.16) | collective-permute-done | bytes 131104 | tf_op jit(solution)/shard_map/ppermute | solution.py:22
  411.0 2.5 fusion.39
  413.6 4.3 multiply_reduce_fusion
  421.3 2.5 fusion.238
  425.5 2.6 fusion.33
  430.0 2.4 convolution_multiply_fusion.2
  432.3 2.3 fusion.67
  436.5 2.7 add_convert_fusion.8
  441.7 4.9 fusion.293
  458.2 2.2 fusion.125
  469.4 2.2 fusion.52
  487.4 2.3 copy.465
  493.6 2.2 copy-done.42
  495.9 2.5 pad_maximum_fusion.1
  501.3 5.6 copy.466
  506.9 2.8 fusion.73
  517.0 3.5 collective-permute-start.29
  526.9 26.2 %collective-permute-done.20 = f32[1,1024]{1,0:T(1,128)S(1)} collective-permute-done((f32[1,1024]{1,0:T(1,128)S(1)}, f32[1,1024]{1,0:T(1,128)S(1)}, u32[]{:S(2)}, u32[]{:S(2)}) %collective-permute-start.20) | collective-permute-done | bytes 4128 | tf_op jit(solution)/shard_map/ppermute | solution.py:22
  555.5 3.4 concatenate.117
  561.5 2.6 bitcast_add_fusion.1
  566.4 2.6 bitcast_add_fusion
  571.7 2.3 bitcast_add_fusion.5
  575.4 4.3 collective-permute-done.21
  583.3 30.2 %collective-permute-done.22 = f32[2,2,64,303]{3,2,1,0:T(8,128)S(1)} collective-permute-done((f32[2,2,64,303]{3,2,1,0:T(8,128)S(1)}, f32[2,2,64,303]{3,2,1,0:T(8,128)S(1)}, u32[]{:S(2)}, u32[]{:S(2)}) %collective-permute-start.22) | collective-permute-done | bytes 310304 | tf_op jit(solution)/shard_map/ppermute | solution.py:76
  613.6 2.7 collective-permute-start.23
  617.4 2.5 collective-permute-done.23
  621.6 5.2 collective-permute-start.24
  646.6 2.8 collective-permute-done.32
  653.6 17.2 %collective-permute-done.28 = bf16[64,1168]{1,0:T(8,128)(2,1)S(1)} collective-permute-done((bf16[64,1168]{1,0:T(8,128)(2,1)S(1)}, bf16[64,1168]{1,0:T(8,128)(2,1)S(1)}, u32[]{:S(2)}, u32[]{:S(2)}) %collective-permute-start.28) | collective-permute-done | bytes 149536 | tf_op jit(solution)/shard_map/ppermute | solution.py:76
  672.6 3.5 collective-permute-start.36
  676.3 13.8 %collective-permute-done.36 = bf16[64,2048]{1,0:T(8,128)(2,1)S(1)} collective-permute-done((bf16[64,2048]{1,0:T(8,128)(2,1)S(1)}, bf16[64,2048]{1,0:T(8,128)(2,1)S(1)}, u32[]{:S(2)}, u32[]{:S(2)}) %collective-permute-start.36) | collective-permute-done | bytes 262176 | tf_op jit(solution)/shard_map/ppermute | solution.py:76
  691.0 4.7 collective-permute-done.40
  (900 shorter events, 280.5 us)
Async XLA Ops:
  7.2 84.0 %all-gather.3.cloned.1.call-start = ((), (), s32[]{:S(2)}) async-start(), calls=%async_computation | async-start | bytes 4456448 | tf_op jit(solution)/shard_map/all_gather | solution.py:283
  12.3 244.7 %all-gather.5.cloned.1.call-start = ((), (), s32[]{:S(2)}) async-start(), calls=%async_computation.1 | async-start | bytes 10027008 | tf_op jit(solution)/shard_map/all_gather | solution.py:287
  14.3 101.3 %copy-start.201 = (s32[128]{0:T(128)}, s32[128]{0:T(128)S(1)}, u32[]{:S(2)}) copy-start(s32[128]{0:T(128)S(1)} %and_select_fusion) | copy-start | bytes 1540
  15.7 88.3 %copy-start.199 = (f32[128]{0:T(128)}, f32[128]{0:T(128)S(1)}, u32[]{:S(2)}) copy-start(f32[128]{0:T(128)S(1)} %broadcast_multiply_fusion.4) | copy-start | bytes 1540
  15.9 88.1 %copy-start.222 = (f32[128]{0:T(128)}, f32[128]{0:T(128)S(1)}, u32[]{:S(2)}) copy-start(f32[128]{0:T(128)S(1)} %fusion.277) | copy-start | bytes 1540
  18.7 84.3 %copy-start.219 = (f32[128]{0:T(128)}, f32[128]{0:T(128)S(1)}, u32[]{:S(2)}) copy-start(f32[128]{0:T(128)S(1)} %mul.806) | copy-start | bytes 1540
  97.0 6.0 collective-permute-start
  113.5 140.4 %copy-start.5 = (f32[128,512]{0,1:T(8,128)}, f32[128,512]{0,1:T(8,128)S(1)}, u32[]{:S(2)}) copy-start(f32[128,512]{0,1:T(8,128)S(1)} %copy.378) | copy-start | bytes 786436
  117.1 75.8 %copy-start.30 = (f32[8,128,64]{1,2,0:T(8,128)}, f32[8,128,64]{1,2,0:T(8,128)S(1)}, u32[]{:S(2)}) copy-start(f32[8,128,64]{1,2,0:T(8,128)S(1)} %get-tuple-element.167) | copy-start | bytes 786436
  153.3 13.6 %collective-permute-start.1 = (f32[8,64,128]{2,1,0:T(8,128)}, f32[8,64,128]{2,1,0:T(8,128)}, u32[]{:S(2)}, u32[]{:S(2)}) collective-permute-start(f32[8,64,128]{2,1,0:T(8,128)} %pad_maximum_fusion.8), channel_id=1, source_target_pairs={{0,2},{2,4},{4,6},{6,8},{8,10},{10,12},{12,14},{14,16},{16,18},{18... | collective-permute-start | bytes 786440 | tf_op jit(solution)/shard_map/ppermute | solution.py:22
  161.7 77.7 %copy-start.183 = (f32[8,64]{1,0:T(8,128)}, f32[8,64]{1,0:T(8,128)S(1)}, u32[]{:S(2)}) copy-start(f32[8,64]{1,0:T(8,128)S(1)} %mul.863) | copy-start | bytes 6148
  163.2 28.3 %copy-start.88 = (f32[8,128,64]{1,2,0:T(8,128)S(1)}, f32[8,128,64]{1,2,0:T(8,128)}, u32[]{:S(2)}) copy-start(f32[8,128,64]{1,2,0:T(8,128)} %copy-done.87) | copy-start | bytes 786436
  168.4 24.5 %copy-start.85 = (f32[8,128,64]{1,2,0:T(8,128)S(1)}, f32[8,128,64]{1,2,0:T(8,128)}, u32[]{:S(2)}) copy-start(f32[8,128,64]{1,2,0:T(8,128)} %copy-done.84) | copy-start | bytes 786436
  168.4 14.9 %collective-permute-start.2 = (f32[8,64,128]{2,1,0:T(8,128)S(1)}, f32[8,64,128]{2,1,0:T(8,128)S(1)}, u32[]{:S(2)}, u32[]{:S(2)}) collective-permute-start(f32[8,64,128]{2,1,0:T(8,128)S(1)} %fusion.56), channel_id=1, source_target_pairs={{0,4},{2,6},{4,8},{6,10},{8,12},{10,14},{12,16},{14,18},{16,20},{1... | collective-permute-start | bytes 786440 | tf_op jit(solution)/shard_map/ppermute | solution.py:22
  175.4 22.3 %copy-start.237 = (pred[128]{0:T(512)(128)(4,1)S(1)}, pred[128]{0:T(512)(128)(4,1)}, u32[]{:S(2)}) copy-start(pred[128]{0:T(512)(128)(4,1)} %broadcast_and_fusion.9) | copy-start | bytes 388
  175.4 22.3 %copy-start.238 = (pred[128]{0:T(512)(128)(4,1)S(1)}, pred[128]{0:T(512)(128)(4,1)}, u32[]{:S(2)}) copy-start(pred[128]{0:T(512)(128)(4,1)} %broadcast_and_fusion.14) | copy-start | bytes 388
  176.9 50.7 %copy-start.130 = (bf16[128,1024]{1,0:T(8,128)(2,1)S(1)}, bf16[128,1024]{1,0:T(8,128)(2,1)}, u32[]{:S(2)}) copy-start(bf16[128,1024]{1,0:T(8,128)(2,1)} %get-tuple-element.116) | copy-start | bytes 786436
  183.6 14.1 %collective-permute-start.3 = (f32[8,64,128]{2,1,0:T(8,128)S(1)}, f32[8,64,128]{2,1,0:T(8,128)S(1)}, u32[]{:S(2)}, u32[]{:S(2)}) collective-permute-start(f32[8,64,128]{2,1,0:T(8,128)S(1)} %select_add_fusion.3), channel_id=1, source_target_pairs={{0,8},{2,10},{4,12},{6,14},{8,16},{10,18},{12,20},{14,22},{16,24},... | collective-permute-start | bytes 786440 | tf_op jit(solution)/shard_map/ppermute | solution.py:22
  198.7 35.6 %collective-permute-start.4 = (f32[8,64,128]{2,1,0:T(8,128)}, f32[8,64,128]{2,1,0:T(8,128)}, u32[]{:S(2)}, u32[]{:S(2)}) collective-permute-start(f32[8,64,128]{2,1,0:T(8,128)} %select_add_fusion.2), channel_id=1, source_target_pairs={{0,16},{2,18},{4,20},{6,22},{8,24},{10,26},{12,28},{14,30},{1,17},... | collective-permute-start | bytes 786440 | tf_op jit(solution)/shard_map/ppermute | solution.py:22
  236.7 6.6 collective-permute-start.5
  258.8 3.0 collective-permute-start.6
  264.3 9.7 %collective-permute-start.7 = (f32[1,1024]{1,0:T(1,128)}, f32[1,1024]{1,0:T(1,128)}, u32[]{:S(2)}, u32[]{:S(2)}) collective-permute-start(f32[1,1024]{1,0:T(1,128)} %slice.542), channel_id=1, source_target_pairs={{0,2},{2,4},{4,6},{6,8},{8,10},{10,12},{12,14},{14,16},{16,18},{18... | collective-permute-start | bytes 12296 | tf_op jit(solution)/shard_map/ppermute | solution.py:22
  284.9 7.3 %collective-permute-start.9 = (f32[128,1024]{1,0:T(8,128)S(1)}, f32[128,1024]{1,0:T(8,128)S(1)}, u32[]{:S(2)}, u32[]{:S(2)}) collective-permute-start(f32[128,1024]{1,0:T(8,128)S(1)} %fusion.6), channel_id=1, source_target_pairs={{0,1},{1,0},{2,3},{3,2},{4,5},{5,4},{6,7},{7,6},{8,9},{9,8},{10,11... | collective-permute-start | bytes 1572872 | tf_op jit(solution)/shard_map/ppermute | solution.py:26
  286.7 13.7 %collective-permute-start.8 = (f32[128,1024]{1,0:T(8,128)S(1)}, f32[128,1024]{1,0:T(8,128)S(1)}, u32[]{:S(2)}, u32[]{:S(2)}) collective-permute-start(f32[128,1024]{1,0:T(8,128)S(1)} %fusion.4), channel_id=1, source_target_pairs={{0,1},{1,0},{2,3},{3,2},{4,5},{5,4},{6,7},{7,6},{8,9},{9,8},{10,11... | collective-permute-start | bytes 1572872 | tf_op jit(solution)/shard_map/ppermute | solution.py:26
  293.9 5.6 collective-permute-start.10
  333.6 11.0 %collective-permute-start.12 = (f32[8,64,128]{2,1,0:T(8,128)S(1)}, f32[8,64,128]{2,1,0:T(8,128)S(1)}, u32[]{:S(2)}, u32[]{:S(2)}) collective-permute-start(f32[8,64,128]{2,1,0:T(8,128)S(1)} %pad_maximum_fusion.9), channel_id=1, source_target_pairs={{2,0},{4,2},{6,4},{8,6},{10,8},{12,10},{14,12},{16,14},{18,16},{20... | collective-permute-start | bytes 786440 | tf_op jit(solution)/shard_map/ppermute | solution.py:22
  344.8 13.0 %collective-permute-start.13 = (f32[8,64,128]{2,1,0:T(8,128)S(1)}, f32[8,64,128]{2,1,0:T(8,128)}, u32[]{:S(2)}, u32[]{:S(2)}) collective-permute-start(f32[8,64,128]{2,1,0:T(8,128)S(1)} %fusion.53), channel_id=1, source_target_pairs={{4,0},{6,2},{8,4},{10,6},{12,8},{14,10},{16,12},{18,14},{20,16},{2... | collective-permute-start | bytes 786440 | tf_op jit(solution)/shard_map/ppermute | solution.py:22
  349.7 20.7 %copy-start.9 = (f32[2,2,1,2,64,2048]{5,4,3,2,1,0:T(8,128)S(1)}, f32[2,2,1,2,64,2048]{5,4,3,2,1,0:T(8,128)}, u32[]{:S(2)}) copy-start(f32[2,2,1,2,64,2048]{5,4,3,2,1,0:T(8,128)} %get-tuple-element.122) | copy-start | bytes 12582916
  349.7 211.3 %collective-permute-start.33 = (bf16[2,2,2,64,2048]{4,3,0,1,2:T(8,128)(2,1)}, bf16[2,2,2,64,2048]{4,3,0,1,2:T(8,128)(2,1)}, u32[]{:S(2)}, u32[]{:S(2)}) collective-permute-start(bf16[2,2,2,64,2048]{4,3,0,1,2:T(8,128)(2,1)} %fusion.25), channel_id=1, source_target_pairs={{0,2},{2,0},{4,6},{6,4},{8,10},{10,8},{12,14},{14,12},{16,18},{18,... | collective-permute-start | bytes 6291464 | tf_op jit(solution)/shard_map/ppermute | solution.py:76
  359.0 9.2 %collective-permute-start.14 = (f32[8,64,128]{2,1,0:T(8,128)S(1)}, f32[8,64,128]{2,1,0:T(8,128)S(1)}, u32[]{:S(2)}, u32[]{:S(2)}) collective-permute-start(f32[8,64,128]{2,1,0:T(8,128)S(1)} %select_add_fusion.1), channel_id=1, source_target_pairs={{8,0},{10,2},{12,4},{14,6},{16,8},{18,10},{20,12},{22,14},{24,16},... | collective-permute-start | bytes 786440 | tf_op jit(solution)/shard_map/ppermute | solution.py:22
  369.1 14.9 %collective-permute-start.15 = (f32[8,64,128]{2,1,0:T(8,128)S(1)}, f32[8,64,128]{2,1,0:T(8,128)S(1)}, u32[]{:S(2)}, u32[]{:S(2)}) collective-permute-start(f32[8,64,128]{2,1,0:T(8,128)S(1)} %select_add_fusion), channel_id=1, source_target_pairs={{16,0},{18,2},{20,4},{22,6},{24,8},{26,10},{28,12},{30,14},{17,1},... | collective-permute-start | bytes 786440 | tf_op jit(solution)/shard_map/ppermute | solution.py:22
  372.3 32.2 %copy-start.99 = (f32[7,8,64,64]{3,2,1,0:T(8,128)S(1)}, f32[7,8,64,64]{3,2,1,0:T(8,128)}, u32[]{:S(2)}) copy-start(f32[7,8,64,64]{3,2,1,0:T(8,128)} %copy-done.98) | copy-start | bytes 2752516
  372.4 194.0 %collective-permute-start.37 = (bf16[2,2,2,64,2048]{4,3,0,1,2:T(8,128)(2,1)}, bf16[2,2,2,64,2048]{4,3,0,1,2:T(8,128)(2,1)}, u32[]{:S(2)}, u32[]{:S(2)}) collective-permute-start(bf16[2,2,2,64,2048]{4,3,0,1,2:T(8,128)(2,1)} %fusion.26), channel_id=1, source_target_pairs={{0,4},{2,6},{4,0},{6,2},{8,12},{10,14},{12,8},{14,10},{16,20},{18,... | collective-permute-start | bytes 6291464 | tf_op jit(solution)/shard_map/ppermute | solution.py:76
  384.5 20.0 %collective-permute-start.16 = (f32[8,64,64]{2,1,0:T(8,128)S(1)}, f32[8,64,64]{2,1,0:T(8,128)S(1)}, u32[]{:S(2)}, u32[]{:S(2)}) collective-permute-start(f32[8,64,64]{2,1,0:T(8,128)S(1)} %fusion.135), channel_id=1, source_target_pairs={{2,0},{4,2},{6,4},{8,6},{10,8},{12,10},{14,12},{16,14},{18,16},{20... | collective-permute-start | bytes 393224 | tf_op jit(solution)/shard_map/ppermute | solution.py:22
  477.3 32.4 %collective-permute-start.17 = (f32[128,288]{0,1:T(8,128)}, f32[128,288]{0,1:T(8,128)}, u32[]{:S(2)}, u32[]{:S(2)}) collective-permute-start(f32[128,288]{0,1:T(8,128)} %pad_maximum_fusion.10), channel_id=1, source_target_pairs={{0,1},{1,0},{2,3},{3,2},{4,5},{5,4},{6,7},{7,6},{8,9},{9,8},{10,11... | collective-permute-start | bytes 442376 | tf_op jit(solution)/shard_map/ppermute | solution.py:26
  480.4 36.6 %collective-permute-start.19 = (f32[128,1024]{1,0:T(8,128)}, f32[128,1024]{1,0:T(8,128)}, u32[]{:S(2)}, u32[]{:S(2)}) collective-permute-start(f32[128,1024]{1,0:T(8,128)} %fusion.78), channel_id=1, source_target_pairs={{0,1},{1,0},{2,3},{3,2},{4,5},{5,4},{6,7},{7,6},{8,9},{9,8},{10,11... | collective-permute-start | bytes 1572872 | tf_op jit(solution)/shard_map/ppermute | solution.py:26
  481.9 40.3 %collective-permute-start.18 = (f32[128,1024]{1,0:T(8,128)S(1)}, f32[128,1024]{1,0:T(8,128)}, u32[]{:S(2)}, u32[]{:S(2)}) collective-permute-start(f32[128,1024]{1,0:T(8,128)S(1)} %fusion.82), channel_id=1, source_target_pairs={{0,1},{1,0},{2,3},{3,2},{4,5},{5,4},{6,7},{7,6},{8,9},{9,8},{10,11... | collective-permute-start | bytes 1572872 | tf_op jit(solution)/shard_map/ppermute | solution.py:26
  509.7 12.7 %collective-permute-start.11 = (f32[128,1024]{1,0:T(8,128)S(1)}, f32[128,1024]{1,0:T(8,128)S(1)}, u32[]{:S(2)}, u32[]{:S(2)}) collective-permute-start(f32[128,1024]{1,0:T(8,128)S(1)} %fusion.86), channel_id=1, source_target_pairs={{0,1},{1,0},{2,3},{3,2},{4,5},{5,4},{6,7},{7,6},{8,9},{9,8},{10,11... | collective-permute-start | bytes 1572872 | tf_op jit(solution)/shard_map/ppermute | solution.py:26
  517.0 54.7 %collective-permute-start.29 = (bf16[2,2,2,64,1024]{4,3,0,1,2:T(8,128)(2,1)}, bf16[2,2,2,64,1024]{4,3,0,1,2:T(8,128)(2,1)}, u32[]{:S(2)}, u32[]{:S(2)}) collective-permute-start(bf16[2,2,2,64,1024]{4,3,0,1,2:T(8,128)(2,1)} %fusion.73), channel_id=1, source_target_pairs={{0,4},{2,6},{4,0},{6,2},{8,12},{10,14},{12,8},{14,10},{16,20},{18,... | collective-permute-start | bytes 3145736 | tf_op jit(solution)/shard_map/ppermute | solution.py:76
  522.1 31.0 %copy-start.200 = (f32[128]{0:T(128)S(1)}, f32[128]{0:T(128)}, u32[]{:S(2)}) copy-start(f32[128]{0:T(128)} %copy-done.199) | copy-start | bytes 1540
  522.1 30.9 %copy-start.213 = (f32[1024]{0:T(1024)S(1)}, f32[1024]{0:T(1024)}, u32[]{:S(2)}) copy-start(f32[1024]{0:T(1024)} %get-tuple-element.68) | copy-start | bytes 12292
  522.1 30.9 %copy-start.214 = (f32[1024]{0:T(1024)S(1)}, f32[1024]{0:T(1024)}, u32[]{:S(2)}) copy-start(f32[1024]{0:T(1024)} %get-tuple-element.69) | copy-start | bytes 12292
  522.2 30.9 %copy-start.215 = (f32[1024]{0:T(1024)S(1)}, f32[1024]{0:T(1024)}, u32[]{:S(2)}) copy-start(f32[1024]{0:T(1024)} %get-tuple-element.70) | copy-start | bytes 12292
  522.2 30.9 %copy-start.216 = (f32[1024]{0:T(1024)S(1)}, f32[1024]{0:T(1024)}, u32[]{:S(2)}) copy-start(f32[1024]{0:T(1024)} %get-tuple-element.71) | copy-start | bytes 12292
  522.2 30.9 %copy-start.217 = (f32[1024]{0:T(1024)S(1)}, f32[1024]{0:T(1024)}, u32[]{:S(2)}) copy-start(f32[1024]{0:T(1024)} %get-tuple-element.72) | copy-start | bytes 12292
  522.2 30.9 %copy-start.218 = (f32[1024]{0:T(1024)S(1)}, f32[1024]{0:T(1024)}, u32[]{:S(2)}) copy-start(f32[1024]{0:T(1024)} %get-tuple-element.73) | copy-start | bytes 12292
  522.2 59.2 %collective-permute-start.25 = (bf16[2,2,2,64,1168]{4,3,2,1,0:T(8,128)(2,1)}, bf16[2,2,2,64,1168]{4,3,2,1,0:T(8,128)(2,1)}, u32[]{:S(2)}, u32[]{:S(2)}) collective-permute-start(bf16[2,2,2,64,1168]{4,3,2,1,0:T(8,128)(2,1)} %fusion.43), channel_id=1, source_target_pairs={{0,2},{2,0},{4,6},{6,4},{8,10},{10,8},{12,14},{14,12},{16,18},{18,... | collective-permute-start | bytes 3588104 | tf_op jit(solution)/shard_map/ppermute | solution.py:76
  524.5 28.6 %collective-permute-start.20 = (f32[1,1024]{1,0:T(1,128)S(1)}, f32[1,1024]{1,0:T(1,128)S(1)}, u32[]{:S(2)}, u32[]{:S(2)}) collective-permute-start(f32[1,1024]{1,0:T(1,128)S(1)} %slice.569), channel_id=1, source_target_pairs={{2,0},{4,2},{6,4},{8,6},{10,8},{12,10},{14,12},{16,14},{18,16},{20... | collective-permute-start | bytes 12296 | tf_op jit(solution)/shard_map/ppermute | solution.py:22
  559.1 20.5 %collective-permute-start.21 = (f32[2,2,2,64,303]{4,3,1,0,2:T(8,128)S(1)}, f32[2,2,2,64,303]{4,3,1,0,2:T(8,128)S(1)}, u32[]{:S(2)}, u32[]{:S(2)}) collective-permute-start(f32[2,2,2,64,303]{4,3,1,0,2:T(8,128)S(1)} %bitcast.814), channel_id=1, source_target_pairs={{0,4},{2,6},{4,0},{6,2},{8,12},{10,14},{12,8},{14,10},{16,20},{18,... | collective-permute-start | bytes 1861640 | tf_op jit(solution)/shard_map/ppermute | solution.py:76
  565.5 75.7 %collective-permute-start.34 = (bf16[2,2,64,2048]{3,2,0,1:T(8,128)(2,1)}, bf16[2,2,64,2048]{3,2,0,1:T(8,128)(2,1)}, u32[]{:S(2)}, u32[]{:S(2)}) collective-permute-start(bf16[2,2,64,2048]{3,2,0,1:T(8,128)(2,1)} %fusion.71), channel_id=1, source_target_pairs={{0,4},{2,6},{4,0},{6,2},{8,12},{10,14},{12,8},{14,10},{16,20},{18,... | collective-permute-start | bytes 3145736 | tf_op jit(solution)/shard_map/ppermute | solution.py:76
  570.2 74.7 %collective-permute-start.38 = (bf16[2,2,64,2048]{3,2,0,1:T(8,128)(2,1)}, bf16[2,2,64,2048]{3,2,0,1:T(8,128)(2,1)}, u32[]{:S(2)}, u32[]{:S(2)}) collective-permute-start(bf16[2,2,64,2048]{3,2,0,1:T(8,128)(2,1)} %fusion.72), channel_id=1, source_target_pairs={{0,2},{2,0},{4,6},{6,4},{8,10},{10,8},{12,14},{14,12},{16,18},{18,... | collective-permute-start | bytes 3145736 | tf_op jit(solution)/shard_map/ppermute | solution.py:76
  574.1 42.2 %collective-permute-start.30 = (bf16[2,2,64,1024]{3,2,0,1:T(8,128)(2,1)S(1)}, bf16[2,2,64,1024]{3,2,0,1:T(8,128)(2,1)S(1)}, u32[]{:S(2)}, u32[]{:S(2)}) collective-permute-start(bf16[2,2,64,1024]{3,2,0,1:T(8,128)(2,1)S(1)} %fusion.101), channel_id=1, source_target_pairs={{0,2},{2,0},{4,6},{6,4},{8,10},{10,8},{12,14},{14,12},{16,18},{18,... | collective-permute-start | bytes 1572872 | tf_op jit(solution)/shard_map/ppermute | solution.py:76
  579.8 33.6 %collective-permute-start.22 = (f32[2,2,64,303]{3,2,1,0:T(8,128)S(1)}, f32[2,2,64,303]{3,2,1,0:T(8,128)S(1)}, u32[]{:S(2)}, u32[]{:S(2)}) collective-permute-start(f32[2,2,64,303]{3,2,1,0:T(8,128)S(1)} %dynamic-slice_bitcast_fusion), channel_id=1, source_target_pairs={{0,2},{2,0},{4,6},{6,4},{8,10},{10,8},{12,14},{14,12},{16,18},{18,... | collective-permute-start | bytes 930824 | tf_op jit(solution)/shard_map/ppermute | solution.py:76
  583.2 53.1 %collective-permute-start.26 = (bf16[2,2,64,1168]{3,2,1,0:T(8,128)(2,1)S(1)}, bf16[2,2,64,1168]{3,2,1,0:T(8,128)(2,1)}, u32[]{:S(2)}, u32[]{:S(2)}) collective-permute-start(bf16[2,2,64,1168]{3,2,1,0:T(8,128)(2,1)S(1)} %fusion.94), channel_id=1, source_target_pairs={{0,4},{2,6},{4,0},{6,2},{8,12},{10,14},{12,8},{14,10},{16,20},{18,... | collective-permute-start | bytes 1794056 | tf_op jit(solution)/shard_map/ppermute | solution.py:76
  613.6 6.3 collective-permute-start.23
  621.6 10.0 %collective-permute-start.24 = (f32[64,303]{0,1:T(8,128)S(1)}, f32[64,303]{0,1:T(8,128)}, u32[]{:S(2)}, u32[]{:S(2)}) collective-permute-start(f32[64,303]{0,1:T(8,128)S(1)} %bitcast.821), channel_id=1, source_target_pairs={{0,16},{2,18},{4,20},{6,22},{8,24},{10,26},{12,28},{14,30},{16,0},... | collective-permute-start | bytes 232712 | tf_op jit(solution)/shard_map/ppermute | solution.py:76
  628.6 9.8 %collective-permute-start.31 = (bf16[2,64,1024]{2,1,0:T(8,128)(2,1)}, bf16[2,64,1024]{2,1,0:T(8,128)(2,1)}, u32[]{:S(2)}, u32[]{:S(2)}) collective-permute-start(bf16[2,64,1024]{2,1,0:T(8,128)(2,1)} %fusion.129), channel_id=1, source_target_pairs={{0,8},{2,10},{4,12},{6,14},{8,0},{10,2},{12,4},{14,6},{16,24},{18,... | collective-permute-start | bytes 786440 | tf_op jit(solution)/shard_map/ppermute | solution.py:76
  637.6 13.4 %collective-permute-start.27 = (bf16[2,64,1168]{2,1,0:T(8,128)(2,1)S(1)}, bf16[2,64,1168]{2,1,0:T(8,128)(2,1)S(1)}, u32[]{:S(2)}, u32[]{:S(2)}) collective-permute-start(bf16[2,64,1168]{2,1,0:T(8,128)(2,1)S(1)} %fusion.119), channel_id=1, source_target_pairs={{0,8},{2,10},{4,12},{6,14},{8,0},{10,2},{12,4},{14,6},{16,24},{18,... | collective-permute-start | bytes 897032 | tf_op jit(solution)/shard_map/ppermute | solution.py:76
  639.5 9.9 %collective-permute-start.32 = (bf16[64,1024]{1,0:T(8,128)(2,1)S(1)}, bf16[64,1024]{1,0:T(8,128)(2,1)S(1)}, u32[]{:S(2)}, u32[]{:S(2)}) collective-permute-start(bf16[64,1024]{1,0:T(8,128)(2,1)S(1)} %fusion.215), channel_id=1, source_target_pairs={{0,16},{2,18},{4,20},{6,22},{8,24},{10,26},{12,28},{14,30},{16,0},... | collective-permute-start | bytes 393224 | tf_op jit(solution)/shard_map/ppermute | solution.py:76
  642.8 29.6 %collective-permute-start.35 = (bf16[2,64,2048]{2,1,0:T(8,128)(2,1)S(1)}, bf16[2,64,2048]{2,1,0:T(8,128)(2,1)S(1)}, u32[]{:S(2)}, u32[]{:S(2)}) collective-permute-start(bf16[2,64,2048]{2,1,0:T(8,128)(2,1)S(1)} %fusion.102), channel_id=1, source_target_pairs={{0,8},{2,10},{4,12},{6,14},{8,0},{10,2},{12,4},{14,6},{16,24},{18,... | collective-permute-start | bytes 1572872 | tf_op jit(solution)/shard_map/ppermute | solution.py:76
  646.5 29.5 %collective-permute-start.39 = (bf16[2,64,2048]{2,1,0:T(8,128)(2,1)S(1)}, bf16[2,64,2048]{2,1,0:T(8,128)(2,1)S(1)}, u32[]{:S(2)}, u32[]{:S(2)}) collective-permute-start(bf16[2,64,2048]{2,1,0:T(8,128)(2,1)S(1)} %fusion.103), channel_id=1, source_target_pairs={{0,8},{2,10},{4,12},{6,14},{8,0},{10,2},{12,4},{14,6},{16,24},{18,... | collective-permute-start | bytes 1572872 | tf_op jit(solution)/shard_map/ppermute | solution.py:76
  651.1 19.7 %collective-permute-start.28 = (bf16[64,1168]{1,0:T(8,128)(2,1)S(1)}, bf16[64,1168]{1,0:T(8,128)(2,1)S(1)}, u32[]{:S(2)}, u32[]{:S(2)}) collective-permute-start(bf16[64,1168]{1,0:T(8,128)(2,1)S(1)} %fusion.212), channel_id=1, source_target_pairs={{0,16},{2,18},{4,20},{6,22},{8,24},{10,26},{12,28},{14,30},{16,0},... | collective-permute-start | bytes 448520 | tf_op jit(solution)/shard_map/ppermute | solution.py:76
  672.6 17.6 %collective-permute-start.36 = (bf16[64,2048]{1,0:T(8,128)(2,1)S(1)}, bf16[64,2048]{1,0:T(8,128)(2,1)S(1)}, u32[]{:S(2)}, u32[]{:S(2)}) collective-permute-start(bf16[64,2048]{1,0:T(8,128)(2,1)S(1)} %fusion.130), channel_id=1, source_target_pairs={{0,16},{2,18},{4,20},{6,22},{8,24},{10,26},{12,28},{14,30},{16,0},... | collective-permute-start | bytes 786440 | tf_op jit(solution)/shard_map/ppermute | solution.py:76
  676.2 19.4 %collective-permute-start.40 = (bf16[64,2048]{1,0:T(8,128)(2,1)S(1)}, bf16[64,2048]{1,0:T(8,128)(2,1)S(1)}, u32[]{:S(2)}, u32[]{:S(2)}) collective-permute-start(bf16[64,2048]{1,0:T(8,128)(2,1)S(1)} %fusion.131), channel_id=1, source_target_pairs={{0,16},{2,18},{4,20},{6,22},{8,24},{10,26},{12,28},{14,30},{16,0},... | collective-permute-start | bytes 786440 | tf_op jit(solution)/shard_map/ppermute | solution.py:76
  (232 other events, 1110.0 us)
Sparse Core Ops, SparseCore 0:
  12.4 78.7 all-gather.2
  94.0 131.2 all-gather.4
